TPU v7x, 128 devices: a whole 4x4x4 slice. The times are simulated.
128 devices in a mesh: gx: 32 (over x, y, z_lo), gy: 4 (over z_hi, core).
Axes of the slice: x: 4, y: 4, z: 4 (z_hi: 2, z_lo: 2; z = z_hi * 2 + z_lo), core: 2. Of those that a mesh axis runs over, the one named last changes fastest.
Arguments:
- permeability: float32 [32768, 1024], P('gx', 'gy'), may hold values from 0.01 to 100
- basis: float32 [256, 8, 256, 256], P('gx', 'gy'), may hold values from 0 to 1, as said below
- support: int32 [256, 8, 256, 256], P('gx', 'gy'), may hold values from 0 to 1, as said below
Outputs:
- smoothed: float32 [256, 8, 256, 256], P('gx', 'gy')
Inputs may be any that keep to these rules, and one draw needn't show every extreme that they name: support is 1 exactly on a rectangle of the box that contains the block's own 128 x 128 cells in its middle and reaches 32 to 64 cells past them on each side, cut to the grid. basis is positive where support is 1 and 0 elsewhere.
All inputs are finite; a program needn't handle non-finite values.
Results may differ from a plain program's by a relative error of at most 0.0003.
Values sent between devices are 32-bit elements; how exact they have to be, the bound alone decides.
No kernel may reach another device: no remote copies, remote signals or barrier semaphores. Data moves between devices by JAX's collectives and lax.ppermute only.
A program may use at most 128 MiB of HBM per device.

v0:
```python
import jax
import jax.numpy as jnp
from jax import lax
from jax.sharding import PartitionSpec as P

B = 128
ITERS = 2


relaxation = 2.0 / 3.0


def shifted(block, axis, distance):
    devices = range(lax.axis_size(axis))
    route = [(i - distance, i) for i in devices if i - distance in devices]
    return lax.ppermute(block, axis, route)


def padded_2(shard, sides, width):
    for axis, dim in sides:
        devices, length = (lax.axis_size(axis), shard.shape[dim])
        up = [(i, (i + 1) % devices) for i in range(devices - 1)]
        down = [(j, i) for i, j in up]
        last = lax.slice_in_dim(shard, length - width, length, axis=dim)
        initial = lax.slice_in_dim(shard, 0, width, axis=dim)
        before = lax.ppermute(last, axis, up)
        after = lax.ppermute(initial, axis, down)
        shard = jnp.concatenate([before, shard, after], axis=dim)
    return shard


def to_wide(extended, count_x, count_y, block):
    tiles = extended.reshape(count_x + 1, block, count_y + 1, block)
    rows = jnp.concatenate([tiles[:-1], tiles[1:]], axis=1)
    return jnp.concatenate([rows[:, :, :-1], rows[:, :, 1:]], axis=3)


def from_wide(boxes, block):
    count_x, count_y = (boxes.shape[0], boxes.shape[2])
    none = (0, 0)
    tiles = jnp.pad(boxes[:, :block, :, :block], ((0, 1), none, (0, 1), none))
    tiles = tiles + jnp.pad(boxes[:, :block, :, block:], ((0, 1), none, (1, 0), none))
    tiles = tiles + jnp.pad(boxes[:, block:, :, :block], ((1, 0), none, (0, 1), none))
    tiles = tiles + jnp.pad(boxes[:, block:, :, block:], ((1, 0), none, (1, 0), none))
    return tiles.reshape((count_x + 1) * block, (count_y + 1) * block)


def harmonic(left, right):
    summed = left + right
    inside = summed > 0
    return jnp.where(inside, 2.0 * left * right / jnp.where(inside, summed, 1.0), 0.0)


def couplings(padded):
    faces_x = harmonic(padded[:-1, 1:-1], padded[1:, 1:-1])
    faces_y = harmonic(padded[1:-1, :-1], padded[1:-1, 1:])
    east = faces_x[1:]
    west = faces_x[:-1]
    north = faces_y[:, 1:]
    south = faces_y[:, :-1]
    diagonal = east + west + north + south
    return (east, west, north, south, jnp.where(diagonal > 0, diagonal, 1.0))


def smooth(basis, inside, east, west, north, south, diagonal):
    none = (0, 0)
    from_east = jnp.pad(basis[:, 1:], (none, (0, 1), none, none))
    from_west = jnp.pad(basis[:, :-1], (none, (1, 0), none, none))
    from_north = jnp.pad(basis[:, :, :, 1:], (none, none, none, (0, 1)))
    from_south = jnp.pad(basis[:, :, :, :-1], (none, none, none, (1, 0)))
    coupled = east * from_east + west * from_west + north * from_north + south * from_south
    return jnp.where(inside, (1.0 - relaxation) * basis + relaxation * coupled / diagonal, 0.0)


def add_ends(field, lower_in, upper_in, width, axis):
    length = field.shape[axis]
    if axis == 0:
        head = field[:width] + lower_in
        middle = field[width : length - width]
        tail = field[length - width :] + upper_in
    else:
        head = field[:, :width] + lower_in
        middle = field[:, width : length - width]
        tail = field[:, length - width :] + upper_in
    return jnp.concatenate([head, middle, tail], axis=axis)


def send_first(strip, offset):
    return shifted(strip, "gx", offset)


def send_second(strip, offset):
    return shifted(strip, "gy", offset)


def local(permeability, basis, support):
    block = B
    margin = block // 2
    count_x, count_y = (basis.shape[0], basis.shape[1])
    padded = padded_2(permeability, (("gx", 0), ("gy", 1)), margin + 1)
    weights = tuple((to_wide(field, count_x, count_y, block) for field in couplings(padded)))
    inside = (support > 0).transpose(0, 2, 1, 3)
    current = basis.transpose(0, 2, 1, 3)
    for step in range(ITERS):
        current = smooth(current, inside, *weights)
        partial_value = from_wide(current, block)
        lower_in = send_first(partial_value[-margin:], 1)
        upper_in = send_first(partial_value[:margin], -1)
        along = add_ends(partial_value[margin:-margin], lower_in, upper_in, margin, 0)
        lower_in = send_second(along[:, -margin:], 1)
        upper_in = send_second(along[:, :margin], -1)
        owned = add_ends(along[:, margin:-margin], lower_in, upper_in, margin, 1)
        summed = padded_2(owned, (("gx", 0), ("gy", 1)), margin)
        summed = jnp.where(summed > 0, summed, 1.0)
        current = current / to_wide(summed, count_x, count_y, block)
    return current.transpose(0, 2, 1, 3)


def solution(mesh):
    placed = (P("gx", "gy"), P("gx", "gy", None, None), P("gx", "gy", None, None))
    return jax.shard_map(
        local, mesh=mesh, in_specs=placed, out_specs=P("gx", "gy", None, None), check_vma=False
    )
```

profile of v0, /device:TPU:7, one launch (start us, length us, event | category | flops | bytes accessed | tf_op | source)
XLA Modules:
  0.0 256.6 jit_solution(5980993823687746138)
XLA Ops:
  1.7 6.3 %collective-permute-start.1 = (f32[65,256]{0,1:T(8,128)S(1)}, f32[65,256]{0,1:T(8,128)S(1)}, u32[]{:S(2)}, u32[]{:S(2)}) collective-permute-start(f32[65,256]{0,1:T(8,128)S(1)} %get-tuple-element.73), channel_id=1, source_target_pairs={{4,0},{8,4},{12,8},{16,12},{20,16},{24,20},{28,24},{32,28},{36,32}... | collective-permute-start | bytes 199688 | tf_op jit(solution)/shard_map/ppermute | solution.py:27
  7.9 1.9 collective-permute-start
  9.9 5.5 %copy.5 = f32[8,2,256,256]{2,0,3,1:T(8,128)} copy(f32[8,2,256,256]{3,2,1,0:T(8,128)} %param.4) | data formatting | bytes 8388608 | tf_op args[1]
  15.4 8.0 %fusion.7 = (f32[8,255,2,256]{1,0,3,2:T(8,128)}, f32[8,255,2,256]{1,0,3,2:T(8,128)}) fusion(f32[8,256,2,256]{1,0,3,2:T(8,128)} %bitcast.119), kind=kLoop, calls=%fused_computation.76 | loop fusion | bytes 16711680 | tf_op jit(solution)/shard_map/slice | solution.py:67
  23.4 5.5 %copy.4 = s32[8,2,256,256]{2,0,3,1:T(8,128)} copy(s32[8,2,256,256]{3,2,1,0:T(8,128)} %param.5) | data formatting | bytes 8388608 | tf_op args[2]
  29.7 6.1 %collective-permute-start.2 = (f32[1154,65]{0,1:T(8,128)S(1)}, f32[1154,65]{0,1:T(8,128)S(1)}, u32[]{:S(2)}, u32[]{:S(2)}) collective-permute-start(f32[1154,65]{0,1:T(8,128)S(1)} %get-tuple-element.63), channel_id=1, source_target_pairs={{0,1},{1,2},{2,3},{4,5},{5,6},{6,7},{8,9},{9,10},{10,11},{12,13},{... | collective-permute-start | bytes 900128 | tf_op jit(solution)/shard_map/ppermute | solution.py:26
  35.8 2.1 collective-permute-start.3
  37.9 7.3 %fusion.8 = (f32[8,256,2,255]{1,0,3,2:T(8,128)}, f32[8,256,2,255]{1,0,3,2:T(8,128)}) fusion(f32[8,256,2,256]{1,0,3,2:T(8,128)} %bitcast.120), kind=kLoop, calls=%fused_computation.77 | loop fusion | bytes 16711680 | tf_op jit(solution)/shard_map/slice | solution.py:69
  60.4 2.9 %fusion.11 = (f32[8,256,2,128]{1,0,3,2:T(8,128)S(1)}, f32[8,256,2,128]{1,0,3,2:T(8,128)S(1)}, f32[8,256,2,128]{1,0,3,2:T(8,128)S(1)}, f32[8,256,2,128]{1,0,3,2:T(8,128)S(1)}) fusion(f32[8,256,3,128]{1,0,3,2:T(8,128)} %constant_dynamic-update-slice_fusion, f32[8,256,3,128]{1,0,3,2:T(8,128)S(1)} %constant_dynamic-update-slice_fusion.2), kind=kLoop, calls=%fused_computation.80 | loop fusion | bytes 16777216 | tf_op jit(solution)/shard_map/slice | solution.py:35
  63.3 2.7 %constant_dynamic-update-slice_fusion.6 = f32[8,256,3,128]{1,0,3,2:T(8,128)S(1)} fusion(f32[8,256,3,128]{1,0,3,2:T(8,128)S(1)} %constant_dynamic-update-slice_fusion.7, f32[8,128,3,128]{1,0,3,2:T(8,128)} %bitcast.134), kind=kLoop, calls=%fused_computation.64 | loop fusion | bytes 3145728 | tf_op jit(solution)/shard_map/concatenate | solution.py:34
  67.3 5.8 %fusion.13 = (f32[8,256,2,128]{1,0,3,2:T(8,128)}, f32[8,256,2,128]{1,0,3,2:T(8,128)}, f32[8,256,2,128]{1,0,3,2:T(8,128)}, f32[8,256,2,128]{1,0,3,2:T(8,128)}) fusion(f32[8,256,3,128]{1,0,3,2:T(8,128)} %constant_dynamic-update-slice_fusion.4, f32[8,256,3,128]{1,0,3,2:T(8,128)S(1)} %constant_dynamic-update-slice_fusion.6), kind=kLoop, calls=%fused_computation.82 | loop fusion | bytes 16777216 | tf_op jit(solution)/shard_map/slice | solution.py:35
  73.2 12.2 %add_select_fusion.1 = (f32[8,256,2,256]{1,0,3,2:T(8,128)S(1)}, pred[8,2,256,256]{2,0,3,1:T(8,128)(4,1)}) fusion(f32[8,256,2,255]{1,0,3,2:T(8,128)} %get-tuple-element.22, f32[8,256,2,255]{1,0,3,2:T(8,128)} %get-tuple-element.21, f32[8,255,2,256]{1,0,3,2:T(8,128)} %get-tuple-element.20, f32[8,255,2,256]{1,0,3,2:T(8,128)} %get-tuple-element.19, ...), kind=kLoop, calls=%fused_computation.12 | loop fusion | flops 18874368 | bytes 51314688 | tf_op jit(solution)/shard_map/jit(_where)/select_n | solution.py:72
  85.7 1.7 copy-done.3
  91.2 6.0 %collective-permute-start.5 = (f32[64,384]{1,0:T(8,128)}, f32[64,384]{1,0:T(8,128)}, u32[]{:S(2)}, u32[]{:S(2)}) collective-permute-start(f32[64,384]{1,0:T(8,128)} %copy.23), channel_id=1, source_target_pairs={{4,0},{8,4},{12,8},{16,12},{20,16},{24,20},{28,24},{32,28},{36,32}... | collective-permute-start | bytes 294920 | tf_op jit(solution)/shard_map/ppermute | solution.py:16
  97.2 1.7 copy.21
  98.9 1.9 collective-permute-start.4
  102.5 5.0 %collective-permute-done.4 = f32[64,384]{1,0:T(8,128)} collective-permute-done((f32[64,384]{1,0:T(8,128)}, f32[64,384]{1,0:T(8,128)}, u32[]{:S(2)}, u32[]{:S(2)}) %collective-permute-start.4) | collective-permute-done | bytes 98336 | tf_op jit(solution)/shard_map/ppermute | solution.py:16
  108.8 6.2 %collective-permute-start.6 = (f32[1024,64]{0,1:T(8,128)S(1)}, f32[1024,64]{0,1:T(8,128)S(1)}, u32[]{:S(2)}, u32[]{:S(2)}) collective-permute-start(f32[1024,64]{0,1:T(8,128)S(1)} %pad_maximum_fusion.13), channel_id=1, source_target_pairs={{0,1},{1,2},{2,3},{4,5},{5,6},{6,7},{8,9},{9,10},{10,11},{12,13},{... | collective-permute-start | bytes 786440 | tf_op jit(solution)/shard_map/ppermute | solution.py:16
  115.0 3.3 %collective-permute-done.6 = f32[1024,64]{0,1:T(8,128)S(1)} collective-permute-done((f32[1024,64]{0,1:T(8,128)S(1)}, f32[1024,64]{0,1:T(8,128)S(1)}, u32[]{:S(2)}, u32[]{:S(2)}) %collective-permute-start.6) | collective-permute-done | bytes 262176 | tf_op jit(solution)/shard_map/ppermute | solution.py:16
  118.5 1.9 collective-permute-start.7
  121.0 10.3 %collective-permute-done.7 = f32[1024,64]{0,1:T(8,128)S(1)} collective-permute-done((f32[1024,64]{0,1:T(8,128)S(1)}, f32[1024,64]{0,1:T(8,128)S(1)}, u32[]{:S(2)}, u32[]{:S(2)}) %collective-permute-start.7) | collective-permute-done | bytes 262176 | tf_op jit(solution)/shard_map/ppermute | solution.py:16
  131.6 1.9 collective-permute-start.9
  133.5 3.4 %collective-permute-start.8 = (f32[64,256]{0,1:T(8,128)S(1)}, f32[64,256]{0,1:T(8,128)S(1)}, u32[]{:S(2)}, u32[]{:S(2)}) collective-permute-start(f32[64,256]{0,1:T(8,128)S(1)} %get-tuple-element.72), channel_id=1, source_target_pairs={{0,4},{4,8},{8,12},{12,16},{16,20},{20,24},{24,28},{28,32},{32,36}... | collective-permute-start | bytes 196616 | tf_op jit(solution)/shard_map/ppermute | solution.py:26
  137.3 4.9 %collective-permute-done.8 = f32[64,256]{0,1:T(8,128)S(1)} collective-permute-done((f32[64,256]{0,1:T(8,128)S(1)}, f32[64,256]{0,1:T(8,128)S(1)}, u32[]{:S(2)}, u32[]{:S(2)}) %collective-permute-start.8) | collective-permute-done | bytes 65568 | tf_op jit(solution)/shard_map/ppermute | solution.py:26
  143.1 1.9 collective-permute-start.10
  145.0 2.4 collective-permute-start.11
  148.7 5.9 %collective-permute-done.11 = f32[1152,64]{0,1:T(8,128)S(1)} collective-permute-done((f32[1152,64]{0,1:T(8,128)S(1)}, f32[1152,64]{0,1:T(8,128)S(1)}, u32[]{:S(2)}, u32[]{:S(2)}) %collective-permute-start.11) | collective-permute-done | bytes 294944 | tf_op jit(solution)/shard_map/ppermute | solution.py:27
  156.3 1.9 copy-done.4
  158.7 4.3 %fusion.5 = (f32[8,256,2,255]{1,0,3,2:T(8,128)}, f32[8,256,2,255]{1,0,3,2:T(8,128)}) fusion(f32[8,256,2,256]{1,0,3,2:T(8,128)S(1)} %maximum_divide_fusion), kind=kLoop, calls=%fused_computation.74 | loop fusion | bytes 16711680 | tf_op jit(solution)/shard_map/slice | solution.py:69
  163.2 4.7 %fusion.4 = (f32[8,255,2,256]{1,0,3,2:T(8,128)}, f32[8,255,2,256]{1,0,3,2:T(8,128)}) fusion(f32[8,256,2,256]{1,0,3,2:T(8,128)S(1)} %maximum_divide_fusion), kind=kLoop, calls=%fused_computation.73 | loop fusion | bytes 16711680 | tf_op jit(solution)/shard_map/slice | solution.py:67
  167.9 16.2 %add_select_fusion = f32[8,256,2,256]{1,0,3,2:T(8,128)} fusion(f32[8,256,2,255]{1,0,3,2:T(8,128)} %get-tuple-element.14, f32[8,256,2,255]{1,0,3,2:T(8,128)} %get-tuple-element.13, f32[8,255,2,256]{1,0,3,2:T(8,128)} %get-tuple-element.12, f32[8,255,2,256]{1,0,3,2:T(8,128)} %get-tuple-element.11, f32[8,256,2,256]{1,0,3,2:T(8,128)} %copy-done, ...), kind=kLoop, calls=%fused_computation.11 | loop fusion | flops 17825792 | bytes 47120384 | tf_op jit(solution)/shard_map/jit(_where)/select_n | solution.py:72
  184.1 2.6 fusion.3
  188.0 1.9 collective-permute-start.12
  189.9 6.4 %collective-permute-start.13 = (f32[64,384]{0,1:T(8,128)S(1)}, f32[64,384]{0,1:T(8,128)S(1)}, u32[]{:S(2)}, u32[]{:S(2)}) collective-permute-start(f32[64,384]{0,1:T(8,128)S(1)} %get-tuple-element.52), channel_id=1, source_target_pairs={{4,0},{8,4},{12,8},{16,12},{20,16},{24,20},{28,24},{32,28},{36,32}... | collective-permute-start | bytes 294920 | tf_op jit(solution)/shard_map/ppermute | solution.py:16
  199.1 2.9 %collective-permute-start.14 = (f32[1024,64]{0,1:T(8,128)S(1)}, f32[1024,64]{0,1:T(8,128)S(1)}, u32[]{:S(2)}, u32[]{:S(2)}) collective-permute-start(f32[1024,64]{0,1:T(8,128)S(1)} %pad_maximum_fusion.11), channel_id=1, source_target_pairs={{0,1},{1,2},{2,3},{4,5},{5,6},{6,7},{8,9},{9,10},{10,11},{12,13},{... | collective-permute-start | bytes 786440 | tf_op jit(solution)/shard_map/ppermute | solution.py:16
  202.0 3.3 %collective-permute-done.14 = f32[1024,64]{0,1:T(8,128)S(1)} collective-permute-done((f32[1024,64]{0,1:T(8,128)S(1)}, f32[1024,64]{0,1:T(8,128)S(1)}, u32[]{:S(2)}, u32[]{:S(2)}) %collective-permute-start.14) | collective-permute-done | bytes 262176 | tf_op jit(solution)/shard_map/ppermute | solution.py:16
  205.6 1.9 collective-permute-start.15
  208.1 7.4 %collective-permute-done.15 = f32[1024,64]{0,1:T(8,128)S(1)} collective-permute-done((f32[1024,64]{0,1:T(8,128)S(1)}, f32[1024,64]{0,1:T(8,128)S(1)}, u32[]{:S(2)}, u32[]{:S(2)}) %collective-permute-start.15) | collective-permute-done | bytes 262176 | tf_op jit(solution)/shard_map/ppermute | solution.py:16
  215.9 6.5 %collective-permute-start.17 = (f32[64,256]{0,1:T(8,128)S(1)}, f32[64,256]{0,1:T(8,128)S(1)}, u32[]{:S(2)}, u32[]{:S(2)}) collective-permute-start(f32[64,256]{0,1:T(8,128)S(1)} %get-tuple-element.69), channel_id=1, source_target_pairs={{4,0},{8,4},{12,8},{16,12},{20,16},{24,20},{28,24},{32,28},{36,32}... | collective-permute-start | bytes 196616 | tf_op jit(solution)/shard_map/ppermute | solution.py:27
  222.4 1.9 collective-permute-start.16
  224.3 6.8 %collective-permute-done.16 = f32[64,256]{0,1:T(8,128)S(1)} collective-permute-done((f32[64,256]{0,1:T(8,128)S(1)}, f32[64,256]{0,1:T(8,128)S(1)}, u32[]{:S(2)}, u32[]{:S(2)}) %collective-permute-start.16) | collective-permute-done | bytes 65568 | tf_op jit(solution)/shard_map/ppermute | solution.py:26
  232.0 3.8 %collective-permute-start.18 = (f32[1152,64]{0,1:T(8,128)S(1)}, f32[1152,64]{0,1:T(8,128)S(1)}, u32[]{:S(2)}, u32[]{:S(2)}) collective-permute-start(f32[1152,64]{0,1:T(8,128)S(1)} %get-tuple-element.65), channel_id=1, source_target_pairs={{0,1},{1,2},{2,3},{4,5},{5,6},{6,7},{8,9},{9,10},{10,11},{12,13},{... | collective-permute-start | bytes 884744 | tf_op jit(solution)/shard_map/ppermute | solution.py:26
  235.7 1.9 collective-permute-start.19
  237.7 1.7 collective-permute-done.18
  239.4 5.9 %collective-permute-done.19 = f32[1152,64]{0,1:T(8,128)S(1)} collective-permute-done((f32[1152,64]{0,1:T(8,128)S(1)}, f32[1152,64]{0,1:T(8,128)S(1)}, u32[]{:S(2)}, u32[]{:S(2)}) %collective-permute-start.19) | collective-permute-done | bytes 294944 | tf_op jit(solution)/shard_map/ppermute | solution.py:27
  247.1 1.8 copy-done.2
  248.9 2.5 fusion
  251.4 5.2 %copy.17 = f32[8,2,256,256]{3,2,1,0:T(8,128)} copy(f32[8,2,256,256]{2,0,3,1:T(8,128)} %fusion) | data formatting | bytes 8388608 | tf_op jit(solution)/shard_map/transpose | solution.py:116
  (116 shorter events, 39.5 us)
Async XLA Ops:
  1.7 27.2 %collective-permute-start.1 = (f32[65,256]{0,1:T(8,128)S(1)}, f32[65,256]{0,1:T(8,128)S(1)}, u32[]{:S(2)}, u32[]{:S(2)}) collective-permute-start(f32[65,256]{0,1:T(8,128)S(1)} %get-tuple-element.73), channel_id=1, source_target_pairs={{4,0},{8,4},{12,8},{16,12},{20,16},{24,20},{28,24},{32,28},{36,32}... | collective-permute-start | bytes 199688 | tf_op jit(solution)/shard_map/ppermute | solution.py:27
  7.9 20.9 %collective-permute-start = (f32[65,256]{0,1:T(8,128)S(1)}, f32[65,256]{0,1:T(8,128)S(1)}, u32[]{:S(2)}, u32[]{:S(2)}) collective-permute-start(f32[65,256]{0,1:T(8,128)S(1)} %get-tuple-element.74), channel_id=1, source_target_pairs={{0,4},{4,8},{8,12},{12,16},{16,20},{20,24},{24,28},{28,32},{32,36}... | collective-permute-start | bytes 199688 | tf_op jit(solution)/shard_map/ppermute | solution.py:26
  29.7 15.4 %collective-permute-start.2 = (f32[1154,65]{0,1:T(8,128)S(1)}, f32[1154,65]{0,1:T(8,128)S(1)}, u32[]{:S(2)}, u32[]{:S(2)}) collective-permute-start(f32[1154,65]{0,1:T(8,128)S(1)} %get-tuple-element.63), channel_id=1, source_target_pairs={{0,1},{1,2},{2,3},{4,5},{5,6},{6,7},{8,9},{9,10},{10,11},{12,13},{... | collective-permute-start | bytes 900128 | tf_op jit(solution)/shard_map/ppermute | solution.py:26
  35.8 10.3 %collective-permute-start.3 = (f32[1154,65]{0,1:T(8,128)S(1)}, f32[1154,65]{0,1:T(8,128)S(1)}, u32[]{:S(2)}, u32[]{:S(2)}) collective-permute-start(f32[1154,65]{0,1:T(8,128)S(1)} %get-tuple-element.64), channel_id=1, source_target_pairs={{1,0},{2,1},{3,2},{5,4},{6,5},{7,6},{9,8},{10,9},{11,10},{13,12},{... | collective-permute-start | bytes 900128 | tf_op jit(solution)/shard_map/ppermute | solution.py:27
  52.2 20.9 %copy-start.5 = (f32[8,256,2,128]{1,0,3,2:T(8,128)}, f32[8,256,2,128]{1,0,3,2:T(8,128)S(1)}, u32[]{:S(2)}) copy-start(f32[8,256,2,128]{1,0,3,2:T(8,128)S(1)} %get-tuple-element.35) | copy-start | bytes 6291460
  52.3 20.8 %copy-start.7 = (f32[8,256,2,128]{1,0,3,2:T(8,128)}, f32[8,256,2,128]{1,0,3,2:T(8,128)S(1)}, u32[]{:S(2)}) copy-start(f32[8,256,2,128]{1,0,3,2:T(8,128)S(1)} %get-tuple-element.36) | copy-start | bytes 6291460
  63.3 9.8 %copy-start.8 = (f32[8,256,2,128]{1,0,3,2:T(8,128)}, f32[8,256,2,128]{1,0,3,2:T(8,128)S(1)}, u32[]{:S(2)}) copy-start(f32[8,256,2,128]{1,0,3,2:T(8,128)S(1)} %get-tuple-element.27) | copy-start | bytes 6291460
  63.3 9.8 %copy-start.9 = (f32[8,256,2,128]{1,0,3,2:T(8,128)}, f32[8,256,2,128]{1,0,3,2:T(8,128)S(1)}, u32[]{:S(2)}) copy-start(f32[8,256,2,128]{1,0,3,2:T(8,128)S(1)} %get-tuple-element.28) | copy-start | bytes 6291460
  63.3 9.8 %copy-start.10 = (f32[8,256,2,128]{1,0,3,2:T(8,128)}, f32[8,256,2,128]{1,0,3,2:T(8,128)S(1)}, u32[]{:S(2)}) copy-start(f32[8,256,2,128]{1,0,3,2:T(8,128)S(1)} %get-tuple-element.75) | copy-start | bytes 6291460
  63.3 9.8 %copy-start.11 = (f32[8,256,2,128]{1,0,3,2:T(8,128)}, f32[8,256,2,128]{1,0,3,2:T(8,128)S(1)}, u32[]{:S(2)}) copy-start(f32[8,256,2,128]{1,0,3,2:T(8,128)S(1)} %get-tuple-element.76) | copy-start | bytes 6291460
  67.3 5.8 %copy-start.1 = (f32[8,2,256,256]{2,0,3,1:T(8,128)S(1)}, f32[8,2,256,256]{2,0,3,1:T(8,128)}, u32[]{:S(2)}) copy-start(f32[8,2,256,256]{2,0,3,1:T(8,128)} %copy.5) | copy-start | bytes 12582916
  85.4 2.0 copy-start.3
  91.2 10.3 %collective-permute-start.5 = (f32[64,384]{1,0:T(8,128)}, f32[64,384]{1,0:T(8,128)}, u32[]{:S(2)}, u32[]{:S(2)}) collective-permute-start(f32[64,384]{1,0:T(8,128)} %copy.23), channel_id=1, source_target_pairs={{4,0},{8,4},{12,8},{16,12},{20,16},{24,20},{28,24},{32,28},{36,32}... | collective-permute-start | bytes 294920 | tf_op jit(solution)/shard_map/ppermute | solution.py:16
  98.9 8.7 %collective-permute-start.4 = (f32[64,384]{1,0:T(8,128)}, f32[64,384]{1,0:T(8,128)}, u32[]{:S(2)}, u32[]{:S(2)}) collective-permute-start(f32[64,384]{1,0:T(8,128)} %copy.21), channel_id=1, source_target_pairs={{0,4},{4,8},{8,12},{12,16},{16,20},{20,24},{24,28},{28,32},{32,36}... | collective-permute-start | bytes 294920 | tf_op jit(solution)/shard_map/ppermute | solution.py:16
  108.8 9.5 %collective-permute-start.6 = (f32[1024,64]{0,1:T(8,128)S(1)}, f32[1024,64]{0,1:T(8,128)S(1)}, u32[]{:S(2)}, u32[]{:S(2)}) collective-permute-start(f32[1024,64]{0,1:T(8,128)S(1)} %pad_maximum_fusion.13), channel_id=1, source_target_pairs={{0,1},{1,2},{2,3},{4,5},{5,6},{6,7},{8,9},{9,10},{10,11},{12,13},{... | collective-permute-start | bytes 786440 | tf_op jit(solution)/shard_map/ppermute | solution.py:16
  118.5 12.8 %collective-permute-start.7 = (f32[1024,64]{0,1:T(8,128)S(1)}, f32[1024,64]{0,1:T(8,128)S(1)}, u32[]{:S(2)}, u32[]{:S(2)}) collective-permute-start(f32[1024,64]{0,1:T(8,128)S(1)} %get-tuple-element.56), channel_id=1, source_target_pairs={{1,0},{2,1},{3,2},{5,4},{6,5},{7,6},{9,8},{10,9},{11,10},{13,12},{... | collective-permute-start | bytes 786440 | tf_op jit(solution)/shard_map/ppermute | solution.py:16
  131.6 5.7 %collective-permute-start.9 = (f32[64,256]{0,1:T(8,128)S(1)}, f32[64,256]{0,1:T(8,128)S(1)}, u32[]{:S(2)}, u32[]{:S(2)}) collective-permute-start(f32[64,256]{0,1:T(8,128)S(1)} %get-tuple-element.71), channel_id=1, source_target_pairs={{4,0},{8,4},{12,8},{16,12},{20,16},{24,20},{28,24},{32,28},{36,32}... | collective-permute-start | bytes 196616 | tf_op jit(solution)/shard_map/ppermute | solution.py:27
  133.5 8.7 %collective-permute-start.8 = (f32[64,256]{0,1:T(8,128)S(1)}, f32[64,256]{0,1:T(8,128)S(1)}, u32[]{:S(2)}, u32[]{:S(2)}) collective-permute-start(f32[64,256]{0,1:T(8,128)S(1)} %get-tuple-element.72), channel_id=1, source_target_pairs={{0,4},{4,8},{8,12},{12,16},{16,20},{20,24},{24,28},{28,32},{32,36}... | collective-permute-start | bytes 196616 | tf_op jit(solution)/shard_map/ppermute | solution.py:26
  143.1 5.6 %collective-permute-start.10 = (f32[1152,64]{0,1:T(8,128)S(1)}, f32[1152,64]{0,1:T(8,128)S(1)}, u32[]{:S(2)}, u32[]{:S(2)}) collective-permute-start(f32[1152,64]{0,1:T(8,128)S(1)} %get-tuple-element.67), channel_id=1, source_target_pairs={{0,1},{1,2},{2,3},{4,5},{5,6},{6,7},{8,9},{9,10},{10,11},{12,13},{... | collective-permute-start | bytes 884744 | tf_op jit(solution)/shard_map/ppermute | solution.py:26
  145.0 9.5 %collective-permute-start.11 = (f32[1152,64]{0,1:T(8,128)S(1)}, f32[1152,64]{0,1:T(8,128)S(1)}, u32[]{:S(2)}, u32[]{:S(2)}) collective-permute-start(f32[1152,64]{0,1:T(8,128)S(1)} %get-tuple-element.68), channel_id=1, source_target_pairs={{1,0},{2,1},{3,2},{5,4},{6,5},{7,6},{9,8},{10,9},{11,10},{13,12},{... | collective-permute-start | bytes 884744 | tf_op jit(solution)/shard_map/ppermute | solution.py:27
  156.0 2.2 copy-start.4
  158.7 4.5 %copy-start = (f32[8,256,2,256]{1,0,3,2:T(8,128)}, f32[8,256,2,256]{1,0,3,2:T(8,128)S(1)}, u32[]{:S(2)}) copy-start(f32[8,256,2,256]{1,0,3,2:T(8,128)S(1)} %maximum_divide_fusion) | copy-start | bytes 12582916
  163.2 4.7 %copy-start.6 = (f32[8,256,2,128]{1,0,3,2:T(8,128)S(1)}, f32[8,256,2,128]{1,0,3,2:T(8,128)}, u32[]{:S(2)}) copy-start(f32[8,256,2,128]{1,0,3,2:T(8,128)} %copy-done.5) | copy-start | bytes 6291460
  163.2 4.7 %copy-start.12 = (pred[8,2,256,256]{2,0,3,1:T(8,128)(4,1)S(1)}, pred[8,2,256,256]{2,0,3,1:T(8,128)(4,1)}, u32[]{:S(2)}) copy-start(pred[8,2,256,256]{2,0,3,1:T(8,128)(4,1)} %get-tuple-element.6) | copy-start | bytes 3145732
  188.0 9.5 %collective-permute-start.12 = (f32[64,384]{0,1:T(8,128)S(1)}, f32[64,384]{0,1:T(8,128)S(1)}, u32[]{:S(2)}, u32[]{:S(2)}) collective-permute-start(f32[64,384]{0,1:T(8,128)S(1)} %get-tuple-element.51), channel_id=1, source_target_pairs={{0,4},{4,8},{8,12},{12,16},{16,20},{20,24},{24,28},{28,32},{32,36}... | collective-permute-start | bytes 294920 | tf_op jit(solution)/shard_map/ppermute | solution.py:16
  189.9 9.0 %collective-permute-start.13 = (f32[64,384]{0,1:T(8,128)S(1)}, f32[64,384]{0,1:T(8,128)S(1)}, u32[]{:S(2)}, u32[]{:S(2)}) collective-permute-start(f32[64,384]{0,1:T(8,128)S(1)} %get-tuple-element.52), channel_id=1, source_target_pairs={{4,0},{8,4},{12,8},{16,12},{20,16},{24,20},{28,24},{32,28},{36,32}... | collective-permute-start | bytes 294920 | tf_op jit(solution)/shard_map/ppermute | solution.py:16
  199.1 6.2 %collective-permute-start.14 = (f32[1024,64]{0,1:T(8,128)S(1)}, f32[1024,64]{0,1:T(8,128)S(1)}, u32[]{:S(2)}, u32[]{:S(2)}) collective-permute-start(f32[1024,64]{0,1:T(8,128)S(1)} %pad_maximum_fusion.11), channel_id=1, source_target_pairs={{0,1},{1,2},{2,3},{4,5},{5,6},{6,7},{8,9},{9,10},{10,11},{12,13},{... | collective-permute-start | bytes 786440 | tf_op jit(solution)/shard_map/ppermute | solution.py:16
  205.6 9.9 %collective-permute-start.15 = (f32[1024,64]{0,1:T(8,128)S(1)}, f32[1024,64]{0,1:T(8,128)S(1)}, u32[]{:S(2)}, u32[]{:S(2)}) collective-permute-start(f32[1024,64]{0,1:T(8,128)S(1)} %get-tuple-element.48), channel_id=1, source_target_pairs={{1,0},{2,1},{3,2},{5,4},{6,5},{7,6},{9,8},{10,9},{11,10},{13,12},{... | collective-permute-start | bytes 786440 | tf_op jit(solution)/shard_map/ppermute | solution.py:16
  215.9 8.5 %collective-permute-start.17 = (f32[64,256]{0,1:T(8,128)S(1)}, f32[64,256]{0,1:T(8,128)S(1)}, u32[]{:S(2)}, u32[]{:S(2)}) collective-permute-start(f32[64,256]{0,1:T(8,128)S(1)} %get-tuple-element.69), channel_id=1, source_target_pairs={{4,0},{8,4},{12,8},{16,12},{20,16},{24,20},{28,24},{32,28},{36,32}... | collective-permute-start | bytes 196616 | tf_op jit(solution)/shard_map/ppermute | solution.py:27
  222.4 8.7 %collective-permute-start.16 = (f32[64,256]{0,1:T(8,128)S(1)}, f32[64,256]{0,1:T(8,128)S(1)}, u32[]{:S(2)}, u32[]{:S(2)}) collective-permute-start(f32[64,256]{0,1:T(8,128)S(1)} %get-tuple-element.70), channel_id=1, source_target_pairs={{0,4},{4,8},{8,12},{12,16},{16,20},{20,24},{24,28},{28,32},{32,36}... | collective-permute-start | bytes 196616 | tf_op jit(solution)/shard_map/ppermute | solution.py:26
  232.0 7.4 %collective-permute-start.18 = (f32[1152,64]{0,1:T(8,128)S(1)}, f32[1152,64]{0,1:T(8,128)S(1)}, u32[]{:S(2)}, u32[]{:S(2)}) collective-permute-start(f32[1152,64]{0,1:T(8,128)S(1)} %get-tuple-element.65), channel_id=1, source_target_pairs={{0,1},{1,2},{2,3},{4,5},{5,6},{6,7},{8,9},{9,10},{10,11},{12,13},{... | collective-permute-start | bytes 884744 | tf_op jit(solution)/shard_map/ppermute | solution.py:26
  235.7 9.5 %collective-permute-start.19 = (f32[1152,64]{0,1:T(8,128)S(1)}, f32[1152,64]{0,1:T(8,128)S(1)}, u32[]{:S(2)}, u32[]{:S(2)}) collective-permute-start(f32[1152,64]{0,1:T(8,128)S(1)} %get-tuple-element.66), channel_id=1, source_target_pairs={{1,0},{2,1},{3,2},{5,4},{6,5},{7,6},{9,8},{10,9},{11,10},{13,12},{... | collective-permute-start | bytes 884744 | tf_op jit(solution)/shard_map/ppermute | solution.py:27
  246.7 2.2 copy-start.2
where the time goes:
time: 258 us; the launch traced here: 257 us
  local copies, waits for them, and re-layouts  87.7 us (34%)
  starting transfers between devices  69.3 us (27%)
  waiting for transfers between devices  59.3 us (23%)
  other arithmetic  39.5 us (15%)
    unnamed x63, local copies, waits for them, and re-layouts  35.5 us
    ppermute x8, waiting for transfers between devices, shifted(): return lax.ppermute(block, axis, route)  31.5 us
    ppermute x8, starting transfers between devices, shifted(): return lax.ppermute(block, axis, route)  29.2 us
    select_n x2, other arithmetic, smooth(): jnp.where(inside, (1.0 - relaxation) * basis + relaxation * coupled / dia...  28.4 us
    ppermute x6, starting transfers between devices, padded_2(): after = lax.ppermute(initial, axis, down)  21.1 us
    ppermute x6, starting transfers between devices, padded_2(): before = lax.ppermute(last, axis, up)  18.9 us
    ppermute x6, waiting for transfers between devices, padded_2(): before = lax.ppermute(last, axis, up)  14.7 us
    ppermute x6, waiting for transfers between devices, padded_2(): after = lax.ppermute(initial, axis, down)  13.2 us
  transfers between devices with their start and end apart: 20, of which 15 were waited for; matrix products, arithmetic and copies ran while one was open for 12% of the time, Pallas kernels for 0%

commit v1 on v0

v1 whole, which is shorter than its diff:
```python
import jax
import jax.numpy as jnp
from jax import lax
from jax.experimental import pallas as pl
from jax.experimental.pallas import tpu as pltpu
from jax.sharding import PartitionSpec as P


F32 = jnp.float32
TINY = 1.1754944e-38
ROWS = 1224
PROWS = 1184
XR = 744
YR = 2720
CR = 480
GUARDS = ((0, 16, 280, 544, 808, 1072, 1216), (0, 144, 408, 672, 936, 1200, 1216))
VMEM_LIMIT = 48 * 1024 * 1024
WEIGH_ROWS = 64
FIRST_ROWS = 64
SECOND_ROWS = 64


def box_row(i):
    return 24 + 264 * (i // 2) if i % 2 == 0 else 152 + 264 * ((i - 1) // 2)


def chunk_rows(k):
    even = 24 + 264 * (k // 2) + 128 * (k % 2)
    odd = 152 + 264 * ((k - 1) // 2) + 128 * ((k - 1) % 2)
    return even, odd


def lanes(rows):
    return lax.broadcasted_iota(jnp.int32, (rows, 128), 1)


def sides():
    sx = 1 - lax.rem(lax.axis_index("gx"), 2)
    sy = 1 - lax.rem(lax.axis_index("gy"), 2)
    return (sx, 1 - sx), (sy, 1 - sy)


def pack_windows(pieces, first):
    rows = pieces[0].shape[0]
    lane = lanes(rows)
    out = jnp.zeros((rows, 128), F32)
    for c, piece in enumerate(pieces):
        turned = pltpu.roll(piece, (4 * c - first) % 128, 1)
        out = jnp.where(lane // 4 == c, turned, out)
    return out


def joined(pv, r, n):
    return jnp.where(lanes(n) < 64, pv[1, r:r + n], pv[0, r:r + n])


def mover(sem):
    moves = []

    def move(src, dst):
        c = pltpu.make_async_copy(src, dst, sem.at[len(moves)])
        c.start()
        moves.append(c)

    return moves, move


def pack_x_kernel(perm, basis, sx_e, sx_o, pv, mid, xfringe, sem, sem_in):
    (xe, xo), _ = sides()
    loads, load = mover(sem_in)
    moves, move = mover(sem)
    for t in (0, 1):
        for h in (0, 1):
            load(perm.at[pl.ds(952 * t, 72), pl.ds(128 * h, 128)], pv.at[t, h])
        for q in (0, 1):
            load(basis.at[7 * t, q, pl.ds(120 * t, 136), pl.ds(128 * (1 - q), 128)], mid.at[t, q, pl.ds(0, 136)])
            load(basis.at[1 + 5 * t, q, pl.ds(248 * t, 8), pl.ds(128 * (1 - q), 128)], mid.at[t, q, pl.ds(136, 8)])
    for t, out in ((xo, sx_o), (xe, sx_e)):
        for j in (0, 1):
            for h in (0, 1):
                at = 144 * (2 * j + h)
                r0 = pl.multiple_of(120 * t, 8)
                r1 = pl.multiple_of(248 * t, 8)
                move(basis.at[7 * t, j, pl.ds(r0, 136), pl.ds(128 * h, 128)], out.at[pl.ds(at, 136)])
                move(basis.at[1 + 5 * t, j, pl.ds(r1, 8), pl.ds(128 * h, 128)], out.at[pl.ds(at + 136, 8)])
        for h in (0, 1):
            r2 = pl.multiple_of(952 * t, 8)
            move(perm.at[pl.ds(r2, 72), pl.ds(128 * h, 128)], out.at[pl.ds(576 + 72 * h, 72)])
    for c in loads:
        c.wait()
    for t in (0, 1):
        for q in (0, 1):
            pieces = [mid[t, q, 8 * c:8 * c + 8] for c in range(18)]
            xfringe[t, 8 * q:8 * q + 8] = pack_windows(pieces, 126)
        xfringe[t, 16:24] = pack_windows([joined(pv[t], 8 * c, 8) for c in range(9)], 62)
    for t, out in ((xo, sx_o), (xe, sx_e)):
        move(xfringe.at[t], out.at[pl.ds(720, 24)])
    for c in moves:
        c.wait()


def pack_y_kernel(perm, basis, after, sy_e, sy_o, pv, mid, fringe, strip, sem, sem_in):
    _, (ye, yo) = sides()
    loads, load = mover(sem_in)
    moves, move = mover(sem)
    for h in (0, 1):
        load(perm.at[:, pl.ds(128 * h, 128)], pv.at[h])
    for q in (0, 1):
        load(basis.at[:, q, :, pl.ds(128 * (1 - q), 128)], mid.at[q])
    for s, out in ((yo, sy_o), (ye, sy_e)):
        lane = pl.multiple_of(s * 128, 128)
        for i in range(8):
            move(basis.at[i, s, :, pl.ds(lane, 128)], out.at[pl.ds(256 * i, 256)])
    for c in loads:
        c.wait()
    lane = lanes(32)
    for p in (0, 1):
        for q in (0, 1):
            pieces = [mid[q, 2 * (c // 8) + p, 32 * (c % 8):32 * (c % 8) + 32] for c in range(32)]
            fringe[32 * (2 * p + q):32 * (2 * p + q) + 32] = pack_windows(pieces, 126)
    fringe[128:160] = pack_windows([joined(pv, 32 * c, 32) for c in range(32)], 62)
    for h in (0, 1):
        for r in range(0, 512, 32):
            low = pv[h, r:r + 32]
            high = pltpu.roll(pv[h, r + 512:r + 544], 64, 1)
            keep = lane >= 64 if h else lane < 64
            strip[h, r:r + 32] = jnp.where(keep, low, high)
    for s, out in ((yo, sy_o), (ye, sy_e)):
        move(fringe.at[pl.ds(0, 128)], out.at[pl.ds(2048, 128)])
        move(strip.at[s], out.at[pl.ds(2176, 512)])
        move(fringe.at[pl.ds(128, 32)], out.at[pl.ds(2688, 32)])
    for c in moves:
        c.wait()


def corner_kernel(rx_e, rx_o, sc_e, sc_o):
    _, (ye, yo) = sides()
    for s, out in ((yo, sc_o), (ye, sc_e)):
        for slot, rx in ((0, rx_e), (1, rx_o)):
            base = 240 * slot
            m = pl.multiple_of(432 * s, 8)
            k = pl.multiple_of(576 + 72 * s, 8)
            out[base:base + 144] = rx[pl.ds(m, 144)]
            out[base + 144:base + 168] = rx[720:744]
            out[base + 168:base + 240] = rx[pl.ds(k, 72)]


def recip(x):
    r = pl.reciprocal(x, approx=True)
    return r * (2.0 - x * r)


def harmonic(a, b):
    return 2.0 * a * b * recip(jnp.maximum(a + b, TINY))


def main_kernel(perm, basis, rx_e, rx_o, ry_e, ry_o, rc_e, rc_o, out,
                a, b, pe, fx, w, pv, ps, fp, xp, cf, cp, res, sem, sem_out):
    (xe, xo), (ye, yo) = sides()
    copies = []

    def load(src, dst):
        c = pltpu.make_async_copy(src, dst, sem.at[len(copies)])
        c.start()
        copies.append(c)

    for h in (0, 1):
        load(perm.at[:, pl.ds(128 * h, 128)], pv.at[h])
    for s, ry in ((ye, ry_e), (yo, ry_o)):
        load(ry.at[pl.ds(2176, 512)], ps.at[s])
        load(ry.at[pl.ds(2048, 128)], fp.at[s, pl.ds(0, 128)])
        load(ry.at[pl.ds(2688, 32)], fp.at[s, pl.ds(128, 32)])
    for t, rx in ((xe, rx_e), (xo, rx_o)):
        load(rx.at[pl.ds(576, 144)], xp.at[t])
    for s, rc in ((ye, rc_e), (yo, rc_o)):
        for slot, t in ((0, xe), (1, xo)):
            load(rc.at[pl.ds(240 * slot + 144, 24)], cf.at[s, t])
            load(rc.at[pl.ds(240 * slot + 168, 72)], cp.at[s, t])
    early = len(copies)
    for i in range(8):
        for j in (0, 1):
            for h in (0, 1):
                load(basis.at[i, j, :, pl.ds(128 * h, 128)], a.at[i % 2, j, j + h, pl.ds(box_row(i), 256)])
        for s, ry in ((ye, ry_e), (yo, ry_o)):
            load(ry.at[pl.ds(256 * i, 256)], a.at[i % 2, 1 - s, 2 * s, pl.ds(box_row(i), 256)])

    def place(src, at, t, q, blk):
        r0 = pl.multiple_of(8 + 1072 * t, 8)
        r1 = pl.multiple_of(8 + 1200 * t, 8)
        load(src.at[pl.ds(at, 136)], a.at[1 - t, q, blk, pl.ds(r0, 136)])
        load(src.at[pl.ds(at + 136, 8)], a.at[t, q, blk, pl.ds(r1, 8)])

    for t, rx in ((xe, rx_e), (xo, rx_o)):
        for j in (0, 1):
            for h in (0, 1):
                place(rx, 144 * (2 * j + h), t, j, j + h)
    for s, rc in ((ye, rc_e), (yo, rc_o)):
        for slot, t in ((0, xe), (1, xo)):
            place(rc, 240 * slot, t, 1 - s, 2 * s)

    zero = jnp.zeros((8, 128), F32)
    for p in (0, 1):
        for q in (0, 1):
            for k in range(4):
                for g in GUARDS[p]:
                    a[p, q, k, g:g + 8] = zero
                    b[p, q, k, g:g + 8] = zero
    for k in range(4):
        pe[k, 0:8] = zero
        pe[k, PROWS - 8:PROWS] = zero
        fx[k, 0:8] = zero

    for c in copies[:early]:
        c.wait()

    def from_left(n):
        return lanes(n) % 4 < 2

    half32, half8 = lanes(32) < 64, lanes(8) < 64

    def fill(at, n, half, left, own0, own1, right):
        u0 = pltpu.roll(own0, 64, 1)
        u1 = pltpu.roll(own1, 64, 1)
        pe[0, at:at + n] = jnp.where(half, left, u0)
        pe[1, at:at + n] = jnp.where(half, u0, u1)
        pe[2, at:at + n] = jnp.where(half, u1, right)

    for r in range(0, 1024, 32):
        left, right = ps[0, r % 512:r % 512 + 32], ps[1, r % 512:r % 512 + 32]
        if r < 512:
            left, right = pltpu.roll(left, 64, 1), pltpu.roll(right, 64, 1)
        fill(80 + r, 32, half32, left, pv[0, r:r + 32], pv[1, r:r + 32], right)
    for t in (0, 1):
        for c in range(9):
            r = 8 * c
            left, right = pltpu.roll(cp[0, t, r:r + 8], 64, 1), pltpu.roll(cp[1, t, r:r + 8], 64, 1)
            fill(8 + 1096 * t + r, 8, half8, left, xp[t, r:r + 8], xp[t, 72 + r:80 + r], right)
        both = jnp.where(from_left(8), cf[0, t, 16:24], cf[1, t, 16:24])
        for c in range(9):
            r = 8 + 1096 * t + 8 * c
            pe[3, r:r + 8] = pltpu.roll(both, (126 - 4 * c) % 128, 1)
        for q in (0, 1):
            both = jnp.where(from_left(8), cf[0, t, 8 * q:8 * q + 8], cf[1, t, 8 * q:8 * q + 8])
            for c in range(18):
                r = 8 + 1072 * t + 8 * c if c < 17 else 8 + 1200 * t
                a[1 - t if c < 17 else t, q, 3, r:r + 8] = pltpu.roll(both, (126 - 4 * c) % 128, 1)
    both = jnp.where(from_left(32), fp[0, 128:160], fp[1, 128:160])
    for c in range(32):
        pe[3, 80 + 32 * c:112 + 32 * c] = pltpu.roll(both, (126 - 4 * c) % 128, 1)
    for p in (0, 1):
        for q in (0, 1):
            n = 32 * (2 * p + q)
            both = jnp.where(from_left(32), fp[0, n:n + 32], fp[1, n:n + 32])
            for c in range(32):
                r = box_row(2 * (c // 8) + p) + 32 * (c % 8)
                a[p, q, 3, r:r + 32] = pltpu.roll(both, (126 - 4 * c) % 128, 1)

    def edges(n):
        lane = lanes(n)
        return lane == 0, lane == 127

    def weigh(r, n):
        first, last = edges(n)
        here = [pe[k, pl.ds(r, n)] for k in range(4)]
        fxs = []
        for k in range(4):
            f = harmonic(here[k], pe[k, pl.ds(r + 1, n)])
            fx[k, pl.ds(r, n)] = f
            fxs.append(f)
        ahead = [pltpu.roll(x, 127, 1) for x in here]
        fys = [harmonic(here[k], jnp.where(last, ahead[(k + 1) % 4], ahead[k])) for k in range(4)]
        behind = [pltpu.roll(x, 1, 1) for x in fys]
        for k in range(4):
            west = fx[k, pl.ds(r - 1, n)]
            south = jnp.where(first, behind[(k + 3) % 4], behind[k])
            total = fxs[k] + west + fys[k] + south
            inv = 2.0 * recip(jnp.maximum(total, TINY))
            w[0, k, pl.ds(r, n)] = fxs[k] * inv
            w[1, k, pl.ds(r, n)] = west * inv
            w[2, k, pl.ds(r, n)] = fys[k] * inv
            w[3, k, pl.ds(r, n)] = south * inv

    def weigh_step(g, carry):
        weigh(pl.multiple_of(24 + WEIGH_ROWS * g, 8), WEIGH_ROWS)
        return carry

    weigh(8, 16)
    lax.fori_loop(0, 1152 // WEIGH_ROWS, weigh_step, 0)
    for c in copies[early:]:
        c.wait()

    def smooth(src, p, q, off, n, ws, blocks):
        first, last = edges(n)
        pairs = ((0, 1), (2, 3)) if q == 0 else ((3, 0), (1, 2))
        got = {}
        for x, y in pairs:
            bx, by = src[p, q, x, pl.ds(off, n)], src[p, q, y, pl.ds(off, n)]
            rx, ry = pltpu.roll(bx, 1, 1), pltpu.roll(by, 1, 1)
            lx, ly = pltpu.roll(bx, 127, 1), pltpu.roll(by, 127, 1)
            near = {
                x: (bx, jnp.where(last, ly, lx), jnp.where(first, 0.0, rx)),
                y: (by, jnp.where(last, 0.0, ly), jnp.where(first, rx, ry)),
            }
            for k in (x, y):
                if k not in blocks:
                    continue
                c, north, south = near[k]
                we, ww, wn, wsouth = ws[k]
                s = c + wn * north + wsouth * south
                s = s + we * src[p, q, k, pl.ds(off + 1, n)] + ww * src[p, q, k, pl.ds(off - 1, n)]
                got[k] = jnp.where(c > 0, s, 0.0)
        return got

    def group(src, wrow, offs, n, blocks):
        ws = {k: [w[d, k, pl.ds(wrow, n)] for d in range(4)] for k in blocks}
        s = {(p, q): smooth(src, p, q, offs[p], n, ws, blocks) for p in (0, 1) for q in (0, 1)}
        done = {}
        for k in blocks:
            total = (s[0, 0][k] + s[0, 1][k]) + (s[1, 0][k] + s[1, 1][k])
            inv = recip(jnp.maximum(total, TINY))
            for p in (0, 1):
                for q in (0, 1):
                    done[p, q, k] = s[p, q][k] * inv
        return done

    def first_pass(wrow, offs, n):
        for (p, q, k), v in group(a, wrow, offs, n, (0, 1, 2, 3)).items():
            b[p, q, k, pl.ds(offs[p], n)] = v

    first_pass(8, (8, 8), 8)
    first_pass(1168, (1208, 1208), 8)
    for k in range(9):
        even, odd = chunk_rows(k)

        def step(g, carry, k=k, even=even, odd=odd):
            r = pl.multiple_of(FIRST_ROWS * g, 8)
            offs = (pl.multiple_of(even + r, 8), pl.multiple_of(odd + r, 8))
            first_pass(pl.multiple_of(16 + 128 * k + r, 8), offs, FIRST_ROWS)
            return carry

        lax.fori_loop(0, 128 // FIRST_ROWS, step, 0)

    stores = []
    for k in range(9):
        even, odd = chunk_rows(k)
        boxes = ((k // 2) * 2, ((k + 1) // 2) * 2 - 1)

        def step(g, carry, k=k, even=even, odd=odd, boxes=boxes):
            r = pl.multiple_of(SECOND_ROWS * g, 8)
            offs = (pl.multiple_of(even + r, 8), pl.multiple_of(odd + r, 8))
            done = group(b, pl.multiple_of(16 + 128 * k + r, 8), offs, SECOND_ROWS, (0, 1, 2))
            for p in (0, 1):
                i = boxes[p]
                if not 0 <= i < 8:
                    continue
                for j in (0, 1):
                    for h in (0, 1):
                        res[i, j, h, pl.ds(128 * (k - i) + r, SECOND_ROWS)] = done[p, j, j + h]
            return carry

        lax.fori_loop(0, 128 // SECOND_ROWS, step, 0)
        if k >= 1:
            for j in (0, 1):
                for h in (0, 1):
                    c = pltpu.make_async_copy(res.at[k - 1, j, h], out.at[k - 1, j, :, pl.ds(128 * h, 128)], sem_out.at[len(stores)])
                    c.start()
                    stores.append(c)
    for c in stores:
        c.wait()


def both_ways(pairs):
    return pairs + [(d, s) for s, d in pairs]


def swap(block, axis, parity):
    n = lax.axis_size(axis)
    return lax.ppermute(block, axis, both_ways([(i, i + 1) for i in range(parity, n - 1, 2)]))


def hbm(n):
    return [pl.BlockSpec(memory_space=pltpu.HBM)] * n


def bundle(rows):
    return jax.ShapeDtypeStruct((rows, 128), F32)


def local(permeability, basis, support):
    params = pltpu.CompilerParams(vmem_limit_bytes=VMEM_LIMIT)
    dma = pltpu.SemaphoreType.DMA
    sx_e, sx_o = pl.pallas_call(
        pack_x_kernel,
        out_shape=[bundle(XR), bundle(XR)],
        in_specs=hbm(2),
        out_specs=hbm(2),
        scratch_shapes=[
            pltpu.VMEM((2, 2, 72, 128), F32),
            pltpu.VMEM((2, 2, 144, 128), F32),
            pltpu.VMEM((2, 24, 128), F32),
            dma((22,)),
            dma((12,)),
        ],
        compiler_params=pltpu.CompilerParams(vmem_limit_bytes=16 * 1024 * 1024),
        name="pack_x",
    )(permeability, basis)
    rx_o = swap(sx_o, "gx", 1)
    rx_e = swap(sx_e, "gx", 0)
    sy_e, sy_o = pl.pallas_call(
        pack_y_kernel,
        out_shape=[bundle(YR), bundle(YR)],
        in_specs=hbm(3),
        out_specs=hbm(2),
        scratch_shapes=[
            pltpu.VMEM((2, 1024, 128), F32),
            pltpu.VMEM((2, 8, 256, 128), F32),
            pltpu.VMEM((160, 128), F32),
            pltpu.VMEM((2, 512, 128), F32),
            dma((22,)),
            dma((4,)),
        ],
        compiler_params=pltpu.CompilerParams(vmem_limit_bytes=16 * 1024 * 1024),
        name="pack_y",
    )(permeability, basis, sx_e)
    ry_o = swap(sy_o, "gy", 1)
    ry_e = swap(sy_e, "gy", 0)
    sc_e, sc_o = pl.pallas_call(
        corner_kernel,
        out_shape=[bundle(CR), bundle(CR)],
        in_specs=[pl.BlockSpec(memory_space=pltpu.VMEM)] * 2,
        out_specs=[pl.BlockSpec(memory_space=pltpu.VMEM)] * 2,
        compiler_params=pltpu.CompilerParams(vmem_limit_bytes=4 * 1024 * 1024),
        name="corner",
    )(rx_e, rx_o)
    rc_o = swap(sc_o, "gy", 1)
    rc_e = swap(sc_e, "gy", 0)
    return pl.pallas_call(
        main_kernel,
        out_shape=jax.ShapeDtypeStruct(basis.shape, F32),
        in_specs=hbm(8),
        out_specs=pl.BlockSpec(memory_space=pltpu.HBM),
        scratch_shapes=[
            pltpu.VMEM((2, 2, 4, ROWS, 128), F32),
            pltpu.VMEM((2, 2, 4, ROWS, 128), F32),
            pltpu.VMEM((4, PROWS, 128), F32),
            pltpu.VMEM((4, PROWS, 128), F32),
            pltpu.VMEM((4, 4, PROWS, 128), F32),
            pltpu.VMEM((2, 1024, 128), F32),
            pltpu.VMEM((2, 512, 128), F32),
            pltpu.VMEM((2, 160, 128), F32),
            pltpu.VMEM((2, 144, 128), F32),
            pltpu.VMEM((2, 2, 24, 128), F32),
            pltpu.VMEM((2, 2, 72, 128), F32),
            pltpu.VMEM((8, 2, 2, 256, 128), F32),
            dma((96,)),
            dma((32,)),
        ],
        compiler_params=params,
        name="smooth",
    )(permeability, basis, rx_e, rx_o, ry_e, ry_o, rc_e, rc_o)


def solution(mesh):
    placed = (P("gx", "gy"), P("gx", "gy", None, None), P("gx", "gy", None, None))
    return jax.shard_map(
        local, mesh=mesh, in_specs=placed, out_specs=P("gx", "gy", None, None), check_vma=False
    )
```

time: 258 us -> 84.3 us (0.33)
  local copies, waits for them, and re-layouts: 87.7 us -> 3.42 us
  starting transfers between devices: 69.3 us -> 15.9 us
  other arithmetic: 39.5 us -> 0 us
  Pallas kernels: 0 us -> 32.2 us
  waiting for transfers between devices: 59.3 us -> 32.3 us
    ppermute x20 -> x6, starting transfers between devices: 69.3 us -> 15.9 us  [swap(): lax.ppermute(block, axis, both_ways([(i, i + 1) for i in range(parity, n...]
    slice x23 -> x0, local copies, waits for them, and re-layouts: 38.6 us -> none  [the longest x2 12.7 us: smooth(): from_east = jnp.pad(basis[:, 1:], (none, (0, 1), none, none))]
    pallas_call x0 -> x4, Pallas kernels: none -> 32.2 us  [the longest x1 29.7 us: local(): pl.pallas_call(main_kernel, out_shape=jax.ShapeDtypeStruct(basis.shape, F...]
    unnamed x63 -> x6, local copies, waits for them, and re-layouts: 35.5 us -> 3.42 us
    select_n x7 -> x0, other arithmetic: 31.3 us -> none  [the longest x2 28.4 us: smooth(): jnp.where(inside, (1.0 - relaxation) * basis + relaxation * coupled / dia...]
    ppermute x20 -> x6, waiting for transfers between devices: 59.3 us -> 32.3 us  [swap(): lax.ppermute(block, axis, both_ways([(i, i + 1) for i in range(parity, n...]
    concatenate x10 -> x0, local copies, waits for them, and re-layouts: 8.13 us -> none  [the longest x7 5.77 us: to_wide(): rows = jnp.concatenate([tiles[:-1], tiles[1:]], axis=1)]
    transpose x1 -> x0, local copies, waits for them, and re-layouts: 5.23 us -> none  [local(): return current.transpose(0, 2, 1, 3)]
  transfers between devices with their start and end apart: 20 -> 6, of which waited for: 15 -> 3; matrix products, arithmetic and copies ran while one was open for 12% -> 0% of each run, Pallas kernels for 0% -> 0%
where the time goes in v1:
time: 84.3 us; the launch traced here: 84.1 us
  waiting for transfers between devices  32.3 us (38%)
  Pallas kernels  32.2 us (38%)
  starting transfers between devices  15.9 us (19%)
  local copies, waits for them, and re-layouts  3.42 us (4%)
    ppermute x6, waiting for transfers between devices, swap(): lax.ppermute(block, axis, both_ways([(i, i + 1) for i in range(parity, n...  32.3 us
    pallas_call x1, Pallas kernels, local(): pl.pallas_call(main_kernel, out_shape=jax.ShapeDtypeStruct(basis.shape, F...  29.7 us
    ppermute x6, starting transfers between devices, swap(): lax.ppermute(block, axis, both_ways([(i, i + 1) for i in range(parity, n...  15.9 us
    unnamed x6, local copies, waits for them, and re-layouts  3.42 us
    pallas_call x1, Pallas kernels, local(): pl.pallas_call(pack_y_kernel, out_shape=[bundle(YR), bundle(YR)], in_spec...  1.81 us
  transfers between devices with their start and end apart: 6, of which 3 were waited for; matrix products, arithmetic and copies ran while one was open for 0% of the time, Pallas kernels for 0%

profile of v1, /device:TPU:7, one launch (start us, length us, event | category | flops | bytes accessed | tf_op | source)
XLA Modules:
  0.0 84.1 jit_solution(17746160567995672264)
XLA Ops:
  0.0 0.0 copy-start
  0.0 2.2 %copy-done = f32[8,2,256,256]{3,2,1,0:T(8,128)S(1)} copy-done((f32[8,2,256,256]{3,2,1,0:T(8,128)S(1)}, f32[8,2,256,256]{3,2,1,0:T(8,128)}, u32[]{:S(2)}) %copy-start) | copy-done | bytes 4194328
  2.2 0.0 copy-start.1
  2.2 1.2 %copy-done.1 = f32[1024,256]{1,0:T(8,128)S(1)} copy-done((f32[1024,256]{1,0:T(8,128)S(1)}, f32[1024,256]{1,0:T(8,128)}, u32[]{:S(2)}) %copy-start.1) | copy-done | bytes 1048600
  3.4 0.7 pack_x.1
  4.2 0.0 copy-start.2
  4.2 1.8 %pack_y.1 = (f32[2720,128]{1,0:T(8,128)S(1)}, f32[2720,128]{1,0:T(8,128)S(1)}) custom-call(f32[1024,256]{1,0:T(8,128)S(1)} %copy-done.1, f32[8,2,256,256]{3,2,1,0:T(8,128)S(1)} %copy-done, f32[744,128]{1,0:T(8,128)S(1)} %get-tuple-element.11.after), custom_call_target="tpu_custom_call" | custom-call | tf_op jit(solution)/shard_map/pack_y/pallas_call | solution.py:409
  6.0 0.8 collective-permute-start.2
  6.7 5.4 %collective-permute-start.3 = (f32[2720,128]{1,0:T(8,128)S(1)}, f32[2720,128]{1,0:T(8,128)S(1)}, u32[]{:S(2)}, u32[]{:S(2)}) collective-permute-start(f32[2720,128]{1,0:T(8,128)S(1)} %get-tuple-element.14), channel_id=1, source_target_pairs={{1,2},{2,1},{5,6},{6,5},{9,10},{10,9},{13,14},{14,13},{17,18},{18,... | collective-permute-start | bytes 4177928 | tf_op jit(solution)/shard_map/ppermute | solution.py:378
  12.2 5.4 %collective-permute-start.1 = (f32[744,128]{1,0:T(8,128)S(1)}, f32[744,128]{1,0:T(8,128)S(1)}, u32[]{:S(2)}, u32[]{:S(2)}) collective-permute-start(f32[744,128]{1,0:T(8,128)S(1)} %get-tuple-element.12), channel_id=1, source_target_pairs={{4,8},{12,16},{20,24},{28,32},{36,40},{44,48},{52,56},{60,64},{68,... | collective-permute-start | bytes 1142792 | tf_op jit(solution)/shard_map/ppermute | solution.py:378
  17.5 0.1 collective-permute-start
  17.6 5.9 %collective-permute-done.1.rx_o = f32[744,128]{1,0:T(8,128)S(1)} collective-permute-done((f32[744,128]{1,0:T(8,128)S(1)}, f32[744,128]{1,0:T(8,128)S(1)}, u32[]{:S(2)}, u32[]{:S(2)}) %collective-permute-start.1) | collective-permute-done | bytes 380960 | tf_op jit(solution)/shard_map/ppermute | solution.py:378
  23.6 21.5 %collective-permute-done.rx_e = f32[744,128]{1,0:T(8,128)S(1)} collective-permute-done((f32[744,128]{1,0:T(8,128)S(1)}, f32[744,128]{1,0:T(8,128)S(1)}, u32[]{:S(2)}, u32[]{:S(2)}) %collective-permute-start) | collective-permute-done | bytes 380960 | tf_op jit(solution)/shard_map/ppermute | solution.py:378
  45.1 0.1 collective-permute-start.4
  45.2 4.2 %collective-permute-start.5 = (f32[480,128]{1,0:T(8,128)S(1)}, f32[480,128]{1,0:T(8,128)S(1)}, u32[]{:S(2)}, u32[]{:S(2)}) collective-permute-start(f32[480,128]{1,0:T(8,128)S(1)} %get-tuple-element.16), channel_id=1, source_target_pairs={{1,2},{2,1},{5,6},{6,5},{9,10},{10,9},{13,14},{14,13},{17,18},{18,... | collective-permute-start | bytes 737288 | tf_op jit(solution)/shard_map/ppermute | solution.py:378
  49.4 0.0 collective-permute-done.4.rc_e
  49.4 4.8 %collective-permute-done.5.rc_o = f32[480,128]{1,0:T(8,128)S(1)} collective-permute-done((f32[480,128]{1,0:T(8,128)S(1)}, f32[480,128]{1,0:T(8,128)S(1)}, u32[]{:S(2)}, u32[]{:S(2)}) %collective-permute-start.5) | collective-permute-done | bytes 245792 | tf_op jit(solution)/shard_map/ppermute | solution.py:378
  54.2 0.0 collective-permute-done.2.ry_e
  54.2 0.0 collective-permute-done.3.ry_o
  54.2 0.0 copy-done.2
  54.2 29.7 %smooth.1 = f32[8,2,256,256]{3,2,1,0:T(8,128)} custom-call(f32[1024,256]{1,0:T(8,128)S(1)} %copy-done.2, f32[8,2,256,256]{3,2,1,0:T(8,128)} %basis.5, f32[744,128]{1,0:T(8,128)S(1)} %collective-permute-done.rx_e, f32[744,128]{1,0:T(8,128)S(1)} %collective-permute-done.1.rx_o, f32[2720,128]{1,0:T(8,128)S(1)} %collective-permute-done.2.ry_e, ...), custom_call_target="tpu_custom_call" | custom-call | tf_op jit(solution)/shard_map/smooth/pallas_call | solution.py:437
  (1 shorter events, 0.0 us)
Async XLA Ops:
  0.0 2.2 %copy-start = (f32[8,2,256,256]{3,2,1,0:T(8,128)S(1)}, f32[8,2,256,256]{3,2,1,0:T(8,128)}, u32[]{:S(2)}) copy-start(f32[8,2,256,256]{3,2,1,0:T(8,128)} %basis.5) | copy-start | bytes 12582916
  2.2 1.2 %copy-start.1 = (f32[1024,256]{1,0:T(8,128)S(1)}, f32[1024,256]{1,0:T(8,128)}, u32[]{:S(2)}) copy-start(f32[1024,256]{1,0:T(8,128)} %perm.5) | copy-start | bytes 3145732
  4.2 50.1 %copy-start.2 = (f32[1024,256]{1,0:T(8,128)S(1)}, f32[1024,256]{1,0:T(8,128)}, u32[]{:S(2)}) copy-start(f32[1024,256]{1,0:T(8,128)} %perm.5) | copy-start | bytes 3145732
  6.0 48.2 %collective-permute-start.2 = (f32[2720,128]{1,0:T(8,128)S(1)}, f32[2720,128]{1,0:T(8,128)S(1)}, u32[]{:S(2)}, u32[]{:S(2)}) collective-permute-start(f32[2720,128]{1,0:T(8,128)S(1)} %get-tuple-element.13), channel_id=1, source_target_pairs={{0,1},{2,3},{1,0},{3,2},{4,5},{6,7},{5,4},{7,6},{8,9},{10,11},{9,8... | collective-permute-start | bytes 4177928 | tf_op jit(solution)/shard_map/ppermute | solution.py:378
  6.7 47.5 %collective-permute-start.3 = (f32[2720,128]{1,0:T(8,128)S(1)}, f32[2720,128]{1,0:T(8,128)S(1)}, u32[]{:S(2)}, u32[]{:S(2)}) collective-permute-start(f32[2720,128]{1,0:T(8,128)S(1)} %get-tuple-element.14), channel_id=1, source_target_pairs={{1,2},{2,1},{5,6},{6,5},{9,10},{10,9},{13,14},{14,13},{17,18},{18,... | collective-permute-start | bytes 4177928 | tf_op jit(solution)/shard_map/ppermute | solution.py:378
  12.2 11.4 %collective-permute-start.1 = (f32[744,128]{1,0:T(8,128)S(1)}, f32[744,128]{1,0:T(8,128)S(1)}, u32[]{:S(2)}, u32[]{:S(2)}) collective-permute-start(f32[744,128]{1,0:T(8,128)S(1)} %get-tuple-element.12), channel_id=1, source_target_pairs={{4,8},{12,16},{20,24},{28,32},{36,40},{44,48},{52,56},{60,64},{68,... | collective-permute-start | bytes 1142792 | tf_op jit(solution)/shard_map/ppermute | solution.py:378
  17.5 27.5 %collective-permute-start = (f32[744,128]{1,0:T(8,128)S(1)}, f32[744,128]{1,0:T(8,128)S(1)}, u32[]{:S(2)}, u32[]{:S(2)}) collective-permute-start(f32[744,128]{1,0:T(8,128)S(1)} %get-tuple-element.11.after), channel_id=1, source_target_pairs={{0,4},{8,12},{16,20},{24,28},{32,36},{40,44},{48,52},{56,60},{64,6... | collective-permute-start | bytes 1142792 | tf_op jit(solution)/shard_map/ppermute | solution.py:378
  45.1 4.3 %collective-permute-start.4 = (f32[480,128]{1,0:T(8,128)S(1)}, f32[480,128]{1,0:T(8,128)S(1)}, u32[]{:S(2)}, u32[]{:S(2)}) collective-permute-start(f32[480,128]{1,0:T(8,128)S(1)} %get-tuple-element.15), channel_id=1, source_target_pairs={{0,1},{2,3},{1,0},{3,2},{4,5},{6,7},{5,4},{7,6},{8,9},{10,11},{9,8... | collective-permute-start | bytes 737288 | tf_op jit(solution)/shard_map/ppermute | solution.py:378
  45.2 9.0 %collective-permute-start.5 = (f32[480,128]{1,0:T(8,128)S(1)}, f32[480,128]{1,0:T(8,128)S(1)}, u32[]{:S(2)}, u32[]{:S(2)}) collective-permute-start(f32[480,128]{1,0:T(8,128)S(1)} %get-tuple-element.16), channel_id=1, source_target_pairs={{1,2},{2,1},{5,6},{6,5},{9,10},{10,9},{13,14},{14,13},{17,18},{18,... | collective-permute-start | bytes 737288 | tf_op jit(solution)/shard_map/ppermute | solution.py:378

commit v2 on v1

--- a/solution.py
+++ b/solution.py
@@ -14,10 +14,12 @@
 YR = 2720
 CR = 480
 GUARDS = ((0, 16, 280, 544, 808, 1072, 1216), (0, 144, 408, 672, 936, 1200, 1216))
-VMEM_LIMIT = 48 * 1024 * 1024
+VMEM_LIMIT = 60 * 1024 * 1024
+SUB = 8
+PACK_LIMIT = 16 * 1024 * 1024
 WEIGH_ROWS = 64
-FIRST_ROWS = 64
-SECOND_ROWS = 64
+FIRST_ROWS = 128
+SECOND_ROWS = 128
 
 
 def box_row(i):
@@ -131,6 +133,10 @@
         move(fringe.at[pl.ds(128, 32)], out.at[pl.ds(2688, 32)])
     for c in moves:
         c.wait()
+
+
+def gate_kernel(y_e, y_o, after, out_e, out_o):
+    pass
 
 
 def corner_kernel(rx_e, rx_o, sc_e, sc_o):
@@ -335,7 +341,8 @@
         def step(g, carry, k=k, even=even, odd=odd):
             r = pl.multiple_of(FIRST_ROWS * g, 8)
             offs = (pl.multiple_of(even + r, 8), pl.multiple_of(odd + r, 8))
-            first_pass(pl.multiple_of(16 + 128 * k + r, 8), offs, FIRST_ROWS)
+            for u in range(0, FIRST_ROWS, SUB):
+                first_pass(pl.multiple_of(16 + 128 * k + r + u, 8), tuple(pl.multiple_of(o + u, 8) for o in offs), SUB)
             return carry
 
         lax.fori_loop(0, 128 // FIRST_ROWS, step, 0)
@@ -348,14 +355,15 @@
         def step(g, carry, k=k, even=even, odd=odd, boxes=boxes):
             r = pl.multiple_of(SECOND_ROWS * g, 8)
             offs = (pl.multiple_of(even + r, 8), pl.multiple_of(odd + r, 8))
-            done = group(b, pl.multiple_of(16 + 128 * k + r, 8), offs, SECOND_ROWS, (0, 1, 2))
-            for p in (0, 1):
-                i = boxes[p]
-                if not 0 <= i < 8:
-                    continue
-                for j in (0, 1):
-                    for h in (0, 1):
-                        res[i, j, h, pl.ds(128 * (k - i) + r, SECOND_ROWS)] = done[p, j, j + h]
+            for u in range(0, SECOND_ROWS, SUB):
+                done = group(b, pl.multiple_of(16 + 128 * k + r + u, 8), tuple(pl.multiple_of(o + u, 8) for o in offs), SUB, (0, 1, 2))
+                for p in (0, 1):
+                    i = boxes[p]
+                    if not 0 <= i < 8:
+                        continue
+                    for j in (0, 1):
+                        for h in (0, 1):
+                            res[i, j, h, pl.ds(128 * (k - i) + r + u, SUB)] = done[p, j, j + h]
             return carry
 
         lax.fori_loop(0, 128 // SECOND_ROWS, step, 0)
@@ -382,6 +390,10 @@
     return [pl.BlockSpec(memory_space=pltpu.HBM)] * n
 
 
+def vmem(n):
+    return [pl.BlockSpec(memory_space=pltpu.VMEM)] * n
+
+
 def bundle(rows):
     return jax.ShapeDtypeStruct((rows, 128), F32)
 
@@ -393,7 +405,7 @@
         pack_x_kernel,
         out_shape=[bundle(XR), bundle(XR)],
         in_specs=hbm(2),
-        out_specs=hbm(2),
+        out_specs=vmem(2),
         scratch_shapes=[
             pltpu.VMEM((2, 2, 72, 128), F32),
             pltpu.VMEM((2, 2, 144, 128), F32),
@@ -401,7 +413,7 @@
             dma((22,)),
             dma((12,)),
         ],
-        compiler_params=pltpu.CompilerParams(vmem_limit_bytes=16 * 1024 * 1024),
+        compiler_params=pltpu.CompilerParams(vmem_limit_bytes=PACK_LIMIT),
         name="pack_x",
     )(permeability, basis)
     rx_o = swap(sx_o, "gx", 1)
@@ -410,7 +422,7 @@
         pack_y_kernel,
         out_shape=[bundle(YR), bundle(YR)],
         in_specs=hbm(3),
-        out_specs=hbm(2),
+        out_specs=vmem(2),
         scratch_shapes=[
             pltpu.VMEM((2, 1024, 128), F32),
             pltpu.VMEM((2, 8, 256, 128), F32),
@@ -419,16 +431,25 @@
             dma((22,)),
             dma((4,)),
         ],
-        compiler_params=pltpu.CompilerParams(vmem_limit_bytes=16 * 1024 * 1024),
+        compiler_params=pltpu.CompilerParams(vmem_limit_bytes=PACK_LIMIT),
         name="pack_y",
     )(permeability, basis, sx_e)
+    sy_e, sy_o = pl.pallas_call(
+        gate_kernel,
+        out_shape=[bundle(YR), bundle(YR)],
+        in_specs=hbm(3),
+        out_specs=hbm(2),
+        input_output_aliases={0: 0, 1: 1},
+        compiler_params=pltpu.CompilerParams(vmem_limit_bytes=1024 * 1024),
+        name="gate",
+    )(sy_e, sy_o, rx_e)
     ry_o = swap(sy_o, "gy", 1)
     ry_e = swap(sy_e, "gy", 0)
     sc_e, sc_o = pl.pallas_call(
         corner_kernel,
         out_shape=[bundle(CR), bundle(CR)],
-        in_specs=[pl.BlockSpec(memory_space=pltpu.VMEM)] * 2,
-        out_specs=[pl.BlockSpec(memory_space=pltpu.VMEM)] * 2,
+        in_specs=vmem(2),
+        out_specs=vmem(2),
         compiler_params=pltpu.CompilerParams(vmem_limit_bytes=4 * 1024 * 1024),
         name="corner",
     )(rx_e, rx_o)

time: 84.3 us -> 71.4 us (0.85)
  waiting for transfers between devices: 32.3 us -> 22.6 us
  Pallas kernels: 32.2 us -> 22.7 us
  starting transfers between devices: 15.9 us -> 19.2 us
  local copies, waits for them, and re-layouts: 3.42 us -> 5.65 us
    ppermute x6, waiting for transfers between devices: 32.3 us -> 22.6 us  [swap(): lax.ppermute(block, axis, both_ways([(i, i + 1) for i in range(parity, n...]
    pallas_call x1, Pallas kernels: 29.7 us -> 20.1 us  [local(): pl.pallas_call(main_kernel, out_shape=jax.ShapeDtypeStruct(basis.shape, F...]
    ppermute x6, starting transfers between devices: 15.9 us -> 19.2 us  [swap(): lax.ppermute(block, axis, both_ways([(i, i + 1) for i in range(parity, n...]
    unnamed x6 -> x16, local copies, waits for them, and re-layouts: 3.42 us -> 5.65 us
  transfers between devices with their start and end apart: 6 -> 6, of which waited for: 3 -> 3; matrix products, arithmetic and copies ran while one was open for 0% -> 0% of each run, Pallas kernels for 0% -> 3%
where the time goes in v2:
time: 71.4 us; the launch traced here: 70.4 us
  Pallas kernels  22.7 us (32%)
  waiting for transfers between devices  22.6 us (32%)
  starting transfers between devices  19.2 us (27%)
  local copies, waits for them, and re-layouts  5.65 us (8%)
    ppermute x6, waiting for transfers between devices, swap(): lax.ppermute(block, axis, both_ways([(i, i + 1) for i in range(parity, n...  22.6 us
    pallas_call x1, Pallas kernels, local(): pl.pallas_call(main_kernel, out_shape=jax.ShapeDtypeStruct(basis.shape, F...  20.1 us
    ppermute x6, starting transfers between devices, swap(): lax.ppermute(block, axis, both_ways([(i, i + 1) for i in range(parity, n...  19.2 us
    unnamed x16, local copies, waits for them, and re-layouts  5.65 us
    pallas_call x1, Pallas kernels, local(): pl.pallas_call(pack_y_kernel, out_shape=[bundle(YR), bundle(YR)], in_spec...  1.8 us
  transfers between devices with their start and end apart: 6, of which 3 were waited for; matrix products, arithmetic and copies ran while one was open for 0% of the time, Pallas kernels for 3%

profile of v2, /device:TPU:7, one launch (start us, length us, event | category | flops | bytes accessed | tf_op | source)
XLA Modules:
  0.0 70.4 jit_solution(12741774853781538181)
XLA Ops:
  0.0 0.0 copy-start
  0.0 2.2 %copy-done = f32[8,2,256,256]{3,2,1,0:T(8,128)S(1)} copy-done((f32[8,2,256,256]{3,2,1,0:T(8,128)S(1)}, f32[8,2,256,256]{3,2,1,0:T(8,128)}, u32[]{:S(2)}) %copy-start) | copy-done | bytes 4194328
  2.2 0.0 copy-start.1
  2.2 1.2 %copy-done.1 = f32[1024,256]{1,0:T(8,128)S(1)} copy-done((f32[1024,256]{1,0:T(8,128)S(1)}, f32[1024,256]{1,0:T(8,128)}, u32[]{:S(2)}) %copy-start.1) | copy-done | bytes 1048600
  3.4 0.7 %pack_x.1 = (f32[744,128]{1,0:T(8,128)S(1)}, f32[744,128]{1,0:T(8,128)S(1)}) custom-call(f32[1024,256]{1,0:T(8,128)S(1)} %copy-done.1, f32[8,2,256,256]{3,2,1,0:T(8,128)S(1)} %copy-done), custom_call_target="tpu_custom_call" | custom-call | tf_op jit(solution)/shard_map/pack_x/pallas_call | solution.py:404
  4.2 1.7 %collective-permute-start = (f32[744,128]{1,0:T(8,128)S(1)}, f32[744,128]{1,0:T(8,128)S(1)}, u32[]{:S(2)}, u32[]{:S(2)}) collective-permute-start(f32[744,128]{1,0:T(8,128)S(1)} %get-tuple-element.13.after), channel_id=1, source_target_pairs={{0,4},{8,12},{16,20},{24,28},{32,36},{40,44},{48,52},{56,60},{64,6... | collective-permute-start | bytes 1142792 | tf_op jit(solution)/shard_map/ppermute | solution.py:386
  5.9 1.8 %pack_y.1 = (f32[2720,128]{1,0:T(8,128)S(1)}, f32[2720,128]{1,0:T(8,128)S(1)}) custom-call(f32[1024,256]{1,0:T(8,128)S(1)} %copy-done.1, f32[8,2,256,256]{3,2,1,0:T(8,128)S(1)} %copy-done, f32[744,128]{1,0:T(8,128)S(1)} %get-tuple-element.13.after), custom_call_target="tpu_custom_call" | custom-call | tf_op jit(solution)/shard_map/pack_y/pallas_call | solution.py:421
  7.7 6.7 %collective-permute-done.after.rx_e = f32[744,128]{1,0:T(8,128)S(1)} collective-permute-done((f32[744,128]{1,0:T(8,128)S(1)}, f32[744,128]{1,0:T(8,128)S(1)}, u32[]{:S(2)}, u32[]{:S(2)}) %collective-permute-start) | collective-permute-done | bytes 380960 | tf_op jit(solution)/shard_map/ppermute | solution.py:386
  14.3 0.0 copy-start.2
  14.3 1.3 %collective-permute-start.2 = (f32[2720,128]{1,0:T(8,128)S(1)}, f32[2720,128]{1,0:T(8,128)S(1)}, u32[]{:S(2)}, u32[]{:S(2)}) collective-permute-start(f32[2720,128]{1,0:T(8,128)S(1)} %get-tuple-element.17), channel_id=1, source_target_pairs={{0,1},{2,3},{1,0},{3,2},{4,5},{6,7},{5,4},{7,6},{8,9},{10,11},{9,8... | collective-permute-start | bytes 4177928 | tf_op jit(solution)/shard_map/ppermute | solution.py:386
  15.7 5.2 %collective-permute-start.3 = (f32[2720,128]{1,0:T(8,128)S(1)}, f32[2720,128]{1,0:T(8,128)S(1)}, u32[]{:S(2)}, u32[]{:S(2)}) collective-permute-start(f32[2720,128]{1,0:T(8,128)S(1)} %get-tuple-element.18), channel_id=1, source_target_pairs={{1,2},{2,1},{5,6},{6,5},{9,10},{10,9},{13,14},{14,13},{17,18},{18,... | collective-permute-start | bytes 4177928 | tf_op jit(solution)/shard_map/ppermute | solution.py:386
  20.9 5.4 %collective-permute-start.1 = (f32[744,128]{1,0:T(8,128)S(1)}, f32[744,128]{1,0:T(8,128)S(1)}, u32[]{:S(2)}, u32[]{:S(2)}) collective-permute-start(f32[744,128]{1,0:T(8,128)S(1)} %get-tuple-element.14), channel_id=1, source_target_pairs={{4,8},{12,16},{20,24},{28,32},{36,40},{44,48},{52,56},{60,64},{68,... | collective-permute-start | bytes 1142792 | tf_op jit(solution)/shard_map/ppermute | solution.py:386
  26.3 6.2 %collective-permute-done.1.rx_o = f32[744,128]{1,0:T(8,128)S(1)} collective-permute-done((f32[744,128]{1,0:T(8,128)S(1)}, f32[744,128]{1,0:T(8,128)S(1)}, u32[]{:S(2)}, u32[]{:S(2)}) %collective-permute-start.1) | collective-permute-done | bytes 380960 | tf_op jit(solution)/shard_map/ppermute | solution.py:386
  32.5 0.0 copy-done.2
  32.5 0.0 copy-start.3
  32.5 0.1 collective-permute-start.4
  32.6 5.4 %collective-permute-start.5 = (f32[480,128]{1,0:T(8,128)S(1)}, f32[480,128]{1,0:T(8,128)S(1)}, u32[]{:S(2)}, u32[]{:S(2)}) collective-permute-start(f32[480,128]{1,0:T(8,128)S(1)} %get-tuple-element.20), channel_id=1, source_target_pairs={{1,2},{2,1},{5,6},{6,5},{9,10},{10,9},{13,14},{14,13},{17,18},{18,... | collective-permute-start | bytes 737288 | tf_op jit(solution)/shard_map/ppermute | solution.py:386
  38.1 0.0 collective-permute-done.4.rc_e
  38.1 0.0 copy-start.6
  38.1 9.8 %collective-permute-done.5.rc_o = f32[480,128]{1,0:T(8,128)S(1)} collective-permute-done((f32[480,128]{1,0:T(8,128)S(1)}, f32[480,128]{1,0:T(8,128)S(1)}, u32[]{:S(2)}, u32[]{:S(2)}) %collective-permute-start.5) | collective-permute-done | bytes 245792 | tf_op jit(solution)/shard_map/ppermute | solution.py:386
  47.8 0.0 copy-start.7
  47.9 0.0 collective-permute-done.2.ry_e
  47.9 0.0 copy-start.4
  47.9 0.0 collective-permute-done.3.ry_o
  47.9 0.0 copy-done.3
  47.9 0.0 copy-done.6
  47.9 0.7 copy-done.7
  48.5 0.5 copy-done.4
  49.0 0.0 copy-start.5
  49.0 1.1 %copy-done.5 = f32[2720,128]{1,0:T(8,128)} copy-done((f32[2720,128]{1,0:T(8,128)}, f32[2720,128]{1,0:T(8,128)S(1)}, u32[]{:S(2)}) %copy-start.5) | copy-done | bytes 1392664
  50.1 20.1 %smooth.1 = f32[8,2,256,256]{3,2,1,0:T(8,128)} custom-call(f32[1024,256]{1,0:T(8,128)} %perm.5, f32[8,2,256,256]{3,2,1,0:T(8,128)} %basis.5, f32[744,128]{1,0:T(8,128)} %copy-done.2, f32[744,128]{1,0:T(8,128)} %copy-done.3, f32[2720,128]{1,0:T(8,128)} %copy-done.4, f32[2720,128]{1,0:T(8,128)} %copy-done.5, f32[480,128]{1,0:T(8,128)} %copy-done.6, ...), custom_call_target="tpu_custom_call" | custom-call | tf_op jit(solution)/shard_map/smooth/pallas_call | solution.py:458
  (2 shorter events, 0.0 us)
Async XLA Ops:
  0.0 2.2 %copy-start = (f32[8,2,256,256]{3,2,1,0:T(8,128)S(1)}, f32[8,2,256,256]{3,2,1,0:T(8,128)}, u32[]{:S(2)}) copy-start(f32[8,2,256,256]{3,2,1,0:T(8,128)} %basis.5) | copy-start | bytes 12582916
  2.2 1.2 %copy-start.1 = (f32[1024,256]{1,0:T(8,128)S(1)}, f32[1024,256]{1,0:T(8,128)}, u32[]{:S(2)}) copy-start(f32[1024,256]{1,0:T(8,128)} %perm.5) | copy-start | bytes 3145732
  4.2 10.2 %collective-permute-start = (f32[744,128]{1,0:T(8,128)S(1)}, f32[744,128]{1,0:T(8,128)S(1)}, u32[]{:S(2)}, u32[]{:S(2)}) collective-permute-start(f32[744,128]{1,0:T(8,128)S(1)} %get-tuple-element.13.after), channel_id=1, source_target_pairs={{0,4},{8,12},{16,20},{24,28},{32,36},{40,44},{48,52},{56,60},{64,6... | collective-permute-start | bytes 1142792 | tf_op jit(solution)/shard_map/ppermute | solution.py:386
  14.3 18.1 %copy-start.2 = (f32[744,128]{1,0:T(8,128)}, f32[744,128]{1,0:T(8,128)S(1)}, u32[]{:S(2)}) copy-start(f32[744,128]{1,0:T(8,128)S(1)} %collective-permute-done.after.rx_e) | copy-start | bytes 1142788
  14.3 33.5 %collective-permute-start.2 = (f32[2720,128]{1,0:T(8,128)S(1)}, f32[2720,128]{1,0:T(8,128)S(1)}, u32[]{:S(2)}, u32[]{:S(2)}) collective-permute-start(f32[2720,128]{1,0:T(8,128)S(1)} %get-tuple-element.17), channel_id=1, source_target_pairs={{0,1},{2,3},{1,0},{3,2},{4,5},{6,7},{5,4},{7,6},{8,9},{10,11},{9,8... | collective-permute-start | bytes 4177928 | tf_op jit(solution)/shard_map/ppermute | solution.py:386
  15.7 32.2 %collective-permute-start.3 = (f32[2720,128]{1,0:T(8,128)S(1)}, f32[2720,128]{1,0:T(8,128)S(1)}, u32[]{:S(2)}, u32[]{:S(2)}) collective-permute-start(f32[2720,128]{1,0:T(8,128)S(1)} %get-tuple-element.18), channel_id=1, source_target_pairs={{1,2},{2,1},{5,6},{6,5},{9,10},{10,9},{13,14},{14,13},{17,18},{18,... | collective-permute-start | bytes 4177928 | tf_op jit(solution)/shard_map/ppermute | solution.py:386
  20.9 11.6 %collective-permute-start.1 = (f32[744,128]{1,0:T(8,128)S(1)}, f32[744,128]{1,0:T(8,128)S(1)}, u32[]{:S(2)}, u32[]{:S(2)}) collective-permute-start(f32[744,128]{1,0:T(8,128)S(1)} %get-tuple-element.14), channel_id=1, source_target_pairs={{4,8},{12,16},{20,24},{28,32},{36,40},{44,48},{52,56},{60,64},{68,... | collective-permute-start | bytes 1142792 | tf_op jit(solution)/shard_map/ppermute | solution.py:386
  32.5 15.4 %copy-start.3 = (f32[744,128]{1,0:T(8,128)}, f32[744,128]{1,0:T(8,128)S(1)}, u32[]{:S(2)}) copy-start(f32[744,128]{1,0:T(8,128)S(1)} %collective-permute-done.1.rx_o) | copy-start | bytes 1142788
  32.5 5.5 %collective-permute-start.4 = (f32[480,128]{1,0:T(8,128)S(1)}, f32[480,128]{1,0:T(8,128)S(1)}, u32[]{:S(2)}, u32[]{:S(2)}) collective-permute-start(f32[480,128]{1,0:T(8,128)S(1)} %get-tuple-element.19), channel_id=1, source_target_pairs={{0,1},{2,3},{1,0},{3,2},{4,5},{6,7},{5,4},{7,6},{8,9},{10,11},{9,8... | collective-permute-start | bytes 737288 | tf_op jit(solution)/shard_map/ppermute | solution.py:386
  32.6 15.2 %collective-permute-start.5 = (f32[480,128]{1,0:T(8,128)S(1)}, f32[480,128]{1,0:T(8,128)S(1)}, u32[]{:S(2)}, u32[]{:S(2)}) collective-permute-start(f32[480,128]{1,0:T(8,128)S(1)} %get-tuple-element.20), channel_id=1, source_target_pairs={{1,2},{2,1},{5,6},{6,5},{9,10},{10,9},{13,14},{14,13},{17,18},{18,... | collective-permute-start | bytes 737288 | tf_op jit(solution)/shard_map/ppermute | solution.py:386
  38.1 9.8 %copy-start.6 = (f32[480,128]{1,0:T(8,128)}, f32[480,128]{1,0:T(8,128)S(1)}, u32[]{:S(2)}) copy-start(f32[480,128]{1,0:T(8,128)S(1)} %collective-permute-done.4.rc_e) | copy-start | bytes 737284
  47.8 0.7 copy-start.7
  47.9 1.2 %copy-start.4 = (f32[2720,128]{1,0:T(8,128)}, f32[2720,128]{1,0:T(8,128)S(1)}, u32[]{:S(2)}) copy-start(f32[2720,128]{1,0:T(8,128)S(1)} %collective-permute-done.2.ry_e) | copy-start | bytes 4177924
  49.0 1.1 %copy-start.5 = (f32[2720,128]{1,0:T(8,128)}, f32[2720,128]{1,0:T(8,128)S(1)}, u32[]{:S(2)}) copy-start(f32[2720,128]{1,0:T(8,128)S(1)} %collective-permute-done.3.ry_o) | copy-start | bytes 4177924

commit v3 on v2

--- a/solution.py
+++ b/solution.py
@@ -17,7 +17,7 @@
 VMEM_LIMIT = 60 * 1024 * 1024
 SUB = 8
 PACK_LIMIT = 16 * 1024 * 1024
-WEIGH_ROWS = 64
+WEIGH_ROWS = 128
 FIRST_ROWS = 128
 SECOND_ROWS = 128
 

time: 71.4 us -> 70.2 us (0.983)
  Pallas kernels: 22.7 us -> 21.4 us
    pallas_call x1, Pallas kernels: 20.1 us -> 18.9 us  [local(): pl.pallas_call(main_kernel, out_shape=jax.ShapeDtypeStruct(basis.shape, F...]
where the time goes in v3:
time: 70.2 us; the launch traced here: 69.1 us
  waiting for transfers between devices  22.6 us (32%)
  Pallas kernels  21.4 us (30%)
  starting transfers between devices  19.2 us (27%)
  local copies, waits for them, and re-layouts  5.65 us (8%)
    ppermute x6, waiting for transfers between devices, swap(): lax.ppermute(block, axis, both_ways([(i, i + 1) for i in range(parity, n...  22.6 us
    ppermute x6, starting transfers between devices, swap(): lax.ppermute(block, axis, both_ways([(i, i + 1) for i in range(parity, n...  19.2 us
    pallas_call x1, Pallas kernels, local(): pl.pallas_call(main_kernel, out_shape=jax.ShapeDtypeStruct(basis.shape, F...  18.9 us
    unnamed x16, local copies, waits for them, and re-layouts  5.65 us
    pallas_call x1, Pallas kernels, local(): pl.pallas_call(pack_y_kernel, out_shape=[bundle(YR), bundle(YR)], in_spec...  1.8 us
  transfers between devices with their start and end apart: 6, of which 3 were waited for; matrix products, arithmetic and copies ran while one was open for 0% of the time, Pallas kernels for 3%

profile of v3, /device:TPU:7, one launch (start us, length us, event | category | flops | bytes accessed | tf_op | source)
XLA Modules:
  0.0 69.1 jit_solution(13930173866690709467)
XLA Ops:
  0.0 0.0 copy-start
  0.0 2.2 %copy-done = f32[8,2,256,256]{3,2,1,0:T(8,128)S(1)} copy-done((f32[8,2,256,256]{3,2,1,0:T(8,128)S(1)}, f32[8,2,256,256]{3,2,1,0:T(8,128)}, u32[]{:S(2)}) %copy-start) | copy-done | bytes 4194328
  2.2 0.0 copy-start.1
  2.2 1.2 %copy-done.1 = f32[1024,256]{1,0:T(8,128)S(1)} copy-done((f32[1024,256]{1,0:T(8,128)S(1)}, f32[1024,256]{1,0:T(8,128)}, u32[]{:S(2)}) %copy-start.1) | copy-done | bytes 1048600
  3.4 0.7 %pack_x.1 = (f32[744,128]{1,0:T(8,128)S(1)}, f32[744,128]{1,0:T(8,128)S(1)}) custom-call(f32[1024,256]{1,0:T(8,128)S(1)} %copy-done.1, f32[8,2,256,256]{3,2,1,0:T(8,128)S(1)} %copy-done), custom_call_target="tpu_custom_call" | custom-call | tf_op jit(solution)/shard_map/pack_x/pallas_call | solution.py:404
  4.2 1.7 %collective-permute-start = (f32[744,128]{1,0:T(8,128)S(1)}, f32[744,128]{1,0:T(8,128)S(1)}, u32[]{:S(2)}, u32[]{:S(2)}) collective-permute-start(f32[744,128]{1,0:T(8,128)S(1)} %get-tuple-element.13.after), channel_id=1, source_target_pairs={{0,4},{8,12},{16,20},{24,28},{32,36},{40,44},{48,52},{56,60},{64,6... | collective-permute-start | bytes 1142792 | tf_op jit(solution)/shard_map/ppermute | solution.py:386
  5.9 1.8 %pack_y.1 = (f32[2720,128]{1,0:T(8,128)S(1)}, f32[2720,128]{1,0:T(8,128)S(1)}) custom-call(f32[1024,256]{1,0:T(8,128)S(1)} %copy-done.1, f32[8,2,256,256]{3,2,1,0:T(8,128)S(1)} %copy-done, f32[744,128]{1,0:T(8,128)S(1)} %get-tuple-element.13.after), custom_call_target="tpu_custom_call" | custom-call | tf_op jit(solution)/shard_map/pack_y/pallas_call | solution.py:421
  7.7 6.7 %collective-permute-done.after.rx_e = f32[744,128]{1,0:T(8,128)S(1)} collective-permute-done((f32[744,128]{1,0:T(8,128)S(1)}, f32[744,128]{1,0:T(8,128)S(1)}, u32[]{:S(2)}, u32[]{:S(2)}) %collective-permute-start) | collective-permute-done | bytes 380960 | tf_op jit(solution)/shard_map/ppermute | solution.py:386
  14.3 0.0 copy-start.2
  14.3 1.3 %collective-permute-start.2 = (f32[2720,128]{1,0:T(8,128)S(1)}, f32[2720,128]{1,0:T(8,128)S(1)}, u32[]{:S(2)}, u32[]{:S(2)}) collective-permute-start(f32[2720,128]{1,0:T(8,128)S(1)} %get-tuple-element.17), channel_id=1, source_target_pairs={{0,1},{2,3},{1,0},{3,2},{4,5},{6,7},{5,4},{7,6},{8,9},{10,11},{9,8... | collective-permute-start | bytes 4177928 | tf_op jit(solution)/shard_map/ppermute | solution.py:386
  15.7 5.2 %collective-permute-start.3 = (f32[2720,128]{1,0:T(8,128)S(1)}, f32[2720,128]{1,0:T(8,128)S(1)}, u32[]{:S(2)}, u32[]{:S(2)}) collective-permute-start(f32[2720,128]{1,0:T(8,128)S(1)} %get-tuple-element.18), channel_id=1, source_target_pairs={{1,2},{2,1},{5,6},{6,5},{9,10},{10,9},{13,14},{14,13},{17,18},{18,... | collective-permute-start | bytes 4177928 | tf_op jit(solution)/shard_map/ppermute | solution.py:386
  20.9 5.4 %collective-permute-start.1 = (f32[744,128]{1,0:T(8,128)S(1)}, f32[744,128]{1,0:T(8,128)S(1)}, u32[]{:S(2)}, u32[]{:S(2)}) collective-permute-start(f32[744,128]{1,0:T(8,128)S(1)} %get-tuple-element.14), channel_id=1, source_target_pairs={{4,8},{12,16},{20,24},{28,32},{36,40},{44,48},{52,56},{60,64},{68,... | collective-permute-start | bytes 1142792 | tf_op jit(solution)/shard_map/ppermute | solution.py:386
  26.3 6.2 %collective-permute-done.1.rx_o = f32[744,128]{1,0:T(8,128)S(1)} collective-permute-done((f32[744,128]{1,0:T(8,128)S(1)}, f32[744,128]{1,0:T(8,128)S(1)}, u32[]{:S(2)}, u32[]{:S(2)}) %collective-permute-start.1) | collective-permute-done | bytes 380960 | tf_op jit(solution)/shard_map/ppermute | solution.py:386
  32.5 0.0 copy-done.2
  32.5 0.0 copy-start.3
  32.5 0.1 collective-permute-start.4
  32.6 5.4 %collective-permute-start.5 = (f32[480,128]{1,0:T(8,128)S(1)}, f32[480,128]{1,0:T(8,128)S(1)}, u32[]{:S(2)}, u32[]{:S(2)}) collective-permute-start(f32[480,128]{1,0:T(8,128)S(1)} %get-tuple-element.20), channel_id=1, source_target_pairs={{1,2},{2,1},{5,6},{6,5},{9,10},{10,9},{13,14},{14,13},{17,18},{18,... | collective-permute-start | bytes 737288 | tf_op jit(solution)/shard_map/ppermute | solution.py:386
  38.1 0.0 collective-permute-done.4.rc_e
  38.1 0.0 copy-start.6
  38.1 9.8 %collective-permute-done.5.rc_o = f32[480,128]{1,0:T(8,128)S(1)} collective-permute-done((f32[480,128]{1,0:T(8,128)S(1)}, f32[480,128]{1,0:T(8,128)S(1)}, u32[]{:S(2)}, u32[]{:S(2)}) %collective-permute-start.5) | collective-permute-done | bytes 245792 | tf_op jit(solution)/shard_map/ppermute | solution.py:386
  47.8 0.0 copy-start.7
  47.9 0.0 collective-permute-done.2.ry_e
  47.9 0.0 copy-start.4
  47.9 0.0 collective-permute-done.3.ry_o
  47.9 0.0 copy-done.3
  47.9 0.0 copy-done.6
  47.9 0.7 copy-done.7
  48.5 0.5 copy-done.4
  49.0 0.0 copy-start.5
  49.0 1.1 %copy-done.5 = f32[2720,128]{1,0:T(8,128)} copy-done((f32[2720,128]{1,0:T(8,128)}, f32[2720,128]{1,0:T(8,128)S(1)}, u32[]{:S(2)}) %copy-start.5) | copy-done | bytes 1392664
  50.1 18.9 %smooth.1 = f32[8,2,256,256]{3,2,1,0:T(8,128)} custom-call(f32[1024,256]{1,0:T(8,128)} %perm.5, f32[8,2,256,256]{3,2,1,0:T(8,128)} %basis.5, f32[744,128]{1,0:T(8,128)} %copy-done.2, f32[744,128]{1,0:T(8,128)} %copy-done.3, f32[2720,128]{1,0:T(8,128)} %copy-done.4, f32[2720,128]{1,0:T(8,128)} %copy-done.5, f32[480,128]{1,0:T(8,128)} %copy-done.6, ...), custom_call_target="tpu_custom_call" | custom-call | tf_op jit(solution)/shard_map/smooth/pallas_call | solution.py:458
  (2 shorter events, 0.0 us)
Async XLA Ops:
  0.0 2.2 %copy-start = (f32[8,2,256,256]{3,2,1,0:T(8,128)S(1)}, f32[8,2,256,256]{3,2,1,0:T(8,128)}, u32[]{:S(2)}) copy-start(f32[8,2,256,256]{3,2,1,0:T(8,128)} %basis.5) | copy-start | bytes 12582916
  2.2 1.2 %copy-start.1 = (f32[1024,256]{1,0:T(8,128)S(1)}, f32[1024,256]{1,0:T(8,128)}, u32[]{:S(2)}) copy-start(f32[1024,256]{1,0:T(8,128)} %perm.5) | copy-start | bytes 3145732
  4.2 10.2 %collective-permute-start = (f32[744,128]{1,0:T(8,128)S(1)}, f32[744,128]{1,0:T(8,128)S(1)}, u32[]{:S(2)}, u32[]{:S(2)}) collective-permute-start(f32[744,128]{1,0:T(8,128)S(1)} %get-tuple-element.13.after), channel_id=1, source_target_pairs={{0,4},{8,12},{16,20},{24,28},{32,36},{40,44},{48,52},{56,60},{64,6... | collective-permute-start | bytes 1142792 | tf_op jit(solution)/shard_map/ppermute | solution.py:386
  14.3 18.1 %copy-start.2 = (f32[744,128]{1,0:T(8,128)}, f32[744,128]{1,0:T(8,128)S(1)}, u32[]{:S(2)}) copy-start(f32[744,128]{1,0:T(8,128)S(1)} %collective-permute-done.after.rx_e) | copy-start | bytes 1142788
  14.3 33.5 %collective-permute-start.2 = (f32[2720,128]{1,0:T(8,128)S(1)}, f32[2720,128]{1,0:T(8,128)S(1)}, u32[]{:S(2)}, u32[]{:S(2)}) collective-permute-start(f32[2720,128]{1,0:T(8,128)S(1)} %get-tuple-element.17), channel_id=1, source_target_pairs={{0,1},{2,3},{1,0},{3,2},{4,5},{6,7},{5,4},{7,6},{8,9},{10,11},{9,8... | collective-permute-start | bytes 4177928 | tf_op jit(solution)/shard_map/ppermute | solution.py:386
  15.7 32.2 %collective-permute-start.3 = (f32[2720,128]{1,0:T(8,128)S(1)}, f32[2720,128]{1,0:T(8,128)S(1)}, u32[]{:S(2)}, u32[]{:S(2)}) collective-permute-start(f32[2720,128]{1,0:T(8,128)S(1)} %get-tuple-element.18), channel_id=1, source_target_pairs={{1,2},{2,1},{5,6},{6,5},{9,10},{10,9},{13,14},{14,13},{17,18},{18,... | collective-permute-start | bytes 4177928 | tf_op jit(solution)/shard_map/ppermute | solution.py:386
  20.9 11.6 %collective-permute-start.1 = (f32[744,128]{1,0:T(8,128)S(1)}, f32[744,128]{1,0:T(8,128)S(1)}, u32[]{:S(2)}, u32[]{:S(2)}) collective-permute-start(f32[744,128]{1,0:T(8,128)S(1)} %get-tuple-element.14), channel_id=1, source_target_pairs={{4,8},{12,16},{20,24},{28,32},{36,40},{44,48},{52,56},{60,64},{68,... | collective-permute-start | bytes 1142792 | tf_op jit(solution)/shard_map/ppermute | solution.py:386
  32.5 15.4 %copy-start.3 = (f32[744,128]{1,0:T(8,128)}, f32[744,128]{1,0:T(8,128)S(1)}, u32[]{:S(2)}) copy-start(f32[744,128]{1,0:T(8,128)S(1)} %collective-permute-done.1.rx_o) | copy-start | bytes 1142788
  32.5 5.5 %collective-permute-start.4 = (f32[480,128]{1,0:T(8,128)S(1)}, f32[480,128]{1,0:T(8,128)S(1)}, u32[]{:S(2)}, u32[]{:S(2)}) collective-permute-start(f32[480,128]{1,0:T(8,128)S(1)} %get-tuple-element.19), channel_id=1, source_target_pairs={{0,1},{2,3},{1,0},{3,2},{4,5},{6,7},{5,4},{7,6},{8,9},{10,11},{9,8... | collective-permute-start | bytes 737288 | tf_op jit(solution)/shard_map/ppermute | solution.py:386
  32.6 15.2 %collective-permute-start.5 = (f32[480,128]{1,0:T(8,128)S(1)}, f32[480,128]{1,0:T(8,128)S(1)}, u32[]{:S(2)}, u32[]{:S(2)}) collective-permute-start(f32[480,128]{1,0:T(8,128)S(1)} %get-tuple-element.20), channel_id=1, source_target_pairs={{1,2},{2,1},{5,6},{6,5},{9,10},{10,9},{13,14},{14,13},{17,18},{18,... | collective-permute-start | bytes 737288 | tf_op jit(solution)/shard_map/ppermute | solution.py:386
  38.1 9.8 %copy-start.6 = (f32[480,128]{1,0:T(8,128)}, f32[480,128]{1,0:T(8,128)S(1)}, u32[]{:S(2)}) copy-start(f32[480,128]{1,0:T(8,128)S(1)} %collective-permute-done.4.rc_e) | copy-start | bytes 737284
  47.8 0.7 copy-start.7
  47.9 1.2 %copy-start.4 = (f32[2720,128]{1,0:T(8,128)}, f32[2720,128]{1,0:T(8,128)S(1)}, u32[]{:S(2)}) copy-start(f32[2720,128]{1,0:T(8,128)S(1)} %collective-permute-done.2.ry_e) | copy-start | bytes 4177924
  49.0 1.1 %copy-start.5 = (f32[2720,128]{1,0:T(8,128)}, f32[2720,128]{1,0:T(8,128)S(1)}, u32[]{:S(2)}) copy-start(f32[2720,128]{1,0:T(8,128)S(1)} %collective-permute-done.3.ry_o) | copy-start | bytes 4177924
